TPU v7x, 32 devices: a whole 2x2x4 slice. The times are simulated.
32 devices in a mesh: lat: 4 (over x, core), lon: 8 (over z, y).
Axes of the slice: x: 2, y: 2, z: 4, core: 2. Of those that a mesh axis runs over, the one named last changes fastest.
Arguments:
- atm_fluxes: bfloat16 [24, 65536], P(None, ('lat', 'lon')), may hold values from -6 to 6
- remap_weights: bfloat16 [32, 64, 128, 128], P(('lat', 'lon')), may hold values from 0 to 0.015625
- source_block: int32 [32, 64], P(('lat', 'lon')), may hold values from 0 to 15
- target_block: int32 [32, 64], P(('lat', 'lon')), may hold values from 0 to 15
- block_count: int32 [32, 32], P(('lat', 'lon')), may hold values from 1 to 2, as said below
- tracers: float32 [6, 16, 64, 1024], P(None, None, 'lat', 'lon'), may hold values from -6 to 6
- east_velocity: float32 [16, 64, 1024], P(None, 'lat', 'lon'), may hold values from -0.3 to 0.3
- north_velocity: float32 [16, 64, 1024], P(None, 'lat', 'lon'), may hold values from -0.3 to 0.3
- land_mask: int32 [64, 1024], P('lat', 'lon'), may hold values 0 or 1
- coupling: float32 [96, 24], replicated, may hold values from -3 to 3
Outputs:
- tracer_out: float32 [6, 16, 64, 1024], P(None, None, 'lat', 'lon')
Inputs may be any that keep to these rules, and one draw needn't show every extreme that they name: Slots 0 to block_count - 1 of a source and tile carry data; in every draw one tile receives all 2 slots from every source.
All inputs are finite; a program needn't handle non-finite values. No bound on the sum of `land_mask` on one device may be relied on, other than what follows from the above.
Results may differ from a plain program's by a relative error of at most 0.0003.
Values sent between devices are 32-bit elements; how exact they have to be, the bound alone decides.
A program may use at most 128 MiB of HBM per device.

v0:
```python
import jax
import jax.numpy as jnp
from jax import lax
from jax.sharding import PartitionSpec as P

NSUB = 4


diffusion_number = 0.2


def extended_2(block, sides, width):
    for axis, dim in sides:
        count = lax.axis_size(axis)
        forward = [(i, i + 1) for i in range(count - 1)]
        forward.append((count - 1, 0))
        backward = [(target, source) for source, target in forward]
        low = lax.ppermute(
            lax.slice_in_dim(block, block.shape[dim] - width, None, axis=dim), axis, forward
        )
        high = lax.ppermute(lax.slice_in_dim(block, 0, width, axis=dim), axis, backward)
        block = jnp.concatenate([low, block, high], axis=dim)
    return block


def advect(tracer_now, east_speed, north_speed, sea_mask):
    mask_east = sea_mask[:, :-1] * sea_mask[:, 1:]
    east_flow = mask_east * (
        east_speed[:, :, :-1] * (tracer_now[..., :-1] + tracer_now[..., 1:]) * 0.5
        - diffusion_number * (tracer_now[..., 1:] - tracer_now[..., :-1])
    )
    mask_north = sea_mask[:-1, :] * sea_mask[1:, :]
    north_flow = mask_north * (
        north_speed[:, :-1, :] * (tracer_now[..., :-1, :] + tracer_now[..., 1:, :]) * 0.5
        - diffusion_number * (tracer_now[..., 1:, :] - tracer_now[..., :-1, :])
    )
    inner = tracer_now[..., 1:-1, 1:-1]
    return (
        inner
        + east_flow[..., 1:-1, :-1]
        - east_flow[..., 1:-1, 1:]
        + north_flow[..., :-1, 1:-1]
        - north_flow[..., 1:, 1:-1]
    )


def split_fields(extended, level_count, rim_depth):
    row_count = extended.shape[1]
    row_ids = jnp.arange(row_count)
    lat_index = lax.axis_index("lat")
    lat_count = lax.axis_size("lat")
    beyond = (lat_index == 0) & (row_ids < rim_depth) | (lat_index == lat_count - 1) & (
        row_ids >= row_count - rim_depth
    )
    sea_mask = jnp.where(beyond[:, None], jnp.float32(0.0), extended[-1])
    return (extended[:level_count], extended[level_count : 2 * level_count], sea_mask)


def per_device(
    atm_fluxes,
    remap_weights,
    source_block,
    target_block,
    block_count,
    tracers,
    east_velocity,
    north_velocity,
    land_mask,
    coupling,
):
    field_count, cell_count = atm_fluxes.shape
    block_cells = remap_weights.shape[-1]
    tile_count = block_count.shape[1]
    slot_count = source_block.shape[1] // tile_count
    tracer_count, level_count, lat_rows, lon_cols = tracers.shape
    atm_blocks = atm_fluxes.reshape(field_count, cell_count // block_cells, block_cells)
    chosen = jnp.take(atm_blocks, source_block[0], axis=1)
    partials = jnp.einsum(
        "fsb,sbc->sfc", chosen, remap_weights[0], preferred_element_type=jnp.float32
    )
    slot_ids = jnp.arange(tile_count * slot_count, dtype=jnp.int32)
    is_live = slot_ids % slot_count < jnp.repeat(block_count[0], slot_count)
    partials = jnp.where(is_live[:, None, None], partials, jnp.float32(0.0))
    targets = jnp.where(is_live, target_block[0], -1).astype(jnp.float32)
    flat_parts = partials.reshape(tile_count, slot_count, field_count * block_cells)
    arrived, landed = (
        lax.all_to_all(flat_parts, ("lat", "lon"), split_axis=0, concat_axis=0, tiled=True),
        lax.all_to_all(
            targets.reshape(tile_count, slot_count),
            ("lat", "lon"),
            split_axis=0,
            concat_axis=0,
            tiled=True,
        ),
    )
    arrived = arrived.reshape(tile_count * slot_count, field_count * block_cells)
    landed = landed.reshape(tile_count * slot_count)
    chooser = (landed[None, :] == jnp.arange(lat_rows, dtype=jnp.float32)[:, None]).astype(
        jnp.float32
    )
    ocean_flux = jnp.dot(
        chooser, arrived, precision=lax.Precision.HIGHEST, preferred_element_type=jnp.float32
    ).reshape(lat_rows, field_count, block_cells)
    source = jnp.einsum(
        "pf,ifj->pij", coupling, ocean_flux, precision=lax.Precision.HIGHEST
    ).reshape(tracer_count, level_count, lat_rows, lon_cols)
    sea_here = land_mask.astype(jnp.float32)
    fields = jnp.concatenate([east_velocity, north_velocity, sea_here[None]], axis=0)
    extended = extended_2(fields, (("lat", 1), ("lon", 2)), 1)
    east_wide, north_wide, mask_wide = split_fields(extended, level_count, 1)
    tracer_now = tracers
    for substep in range(NSUB):
        padded = extended_2(tracer_now, (("lat", 2), ("lon", 3)), 1)
        tracer_now = advect(padded, east_wide, north_wide, mask_wide)
    return tracer_now + sea_here * source


def solution(mesh):
    placed = (
        P(None, ("lat", "lon")),
        P(("lat", "lon"), None, None, None),
        P(("lat", "lon"), None),
        P(("lat", "lon"), None),
        P(("lat", "lon"), None),
        P(None, None, "lat", "lon"),
        P(None, "lat", "lon"),
        P(None, "lat", "lon"),
        P("lat", "lon"),
        P(),
    )
    return jax.shard_map(
        per_device,
        mesh=mesh,
        in_specs=placed,
        out_specs=P(None, None, "lat", "lon"),
        check_vma=False,
    )
```

profile of v0, /device:TPU:0, one launch (start us, length us, event | category | flops | bytes accessed | tf_op | source)
XLA Modules:
  0.0 197.1 jit_solution(13769600055185015958)
XLA Ops:
  0.0 1.3 fusion.32
  2.0 2.4 %collective-permute-start.5 = (f32[6,16,1,128]{3,1,2,0:T(8,128)}, f32[6,16,1,128]{3,1,2,0:T(8,128)}, u32[]{:S(2)}, u32[]{:S(2)}) collective-permute-start(f32[6,16,1,128]{3,1,2,0:T(8,128)} %copy.169), channel_id=1, source_target_pairs={{8,0},{16,8},{24,16},{0,24},{9,1},{17,9},{25,17},{1,25},{10,2},{18... | collective-permute-start | bytes 147464 | tf_op jit(solution)/shard_map/ppermute | solution.py:21
  5.0 1.3 fusion.34
  7.2 1.8 collective-permute-start.1
  9.5 1.3 reduce.6
  12.4 6.2 %all-to-all-start = ((f32[32,1,2]{2,1,0:T(1,128)}), f32[32,1,2]{2,1,0:T(1,128)}, u32[]{:S(2)}, u32[]{:S(2)}) async-start(f32[32,1,2]{2,1,0:T(1,128)} %copy.144), calls=%async_computation | async-start | bytes 32768 | tf_op jit(solution)/shard_map/all_to_all | solution.py:88
  18.7 1.5 copy_bitcast_fusion
  22.3 4.5 %collective-permute-start.3 = (f32[33,18,1]{2,1,0:T(8,128)}, f32[33,18,1]{2,1,0:T(8,128)}, u32[]{:S(2)}, u32[]{:S(2)}) collective-permute-start(f32[33,18,1]{2,1,0:T(8,128)} %get-tuple-element.22), channel_id=1, source_target_pairs={{1,0},{2,1},{3,2},{4,3},{5,4},{6,5},{7,6},{0,7},{9,8},{10,9},{11,1... | collective-permute-start | bytes 7136 | tf_op jit(solution)/shard_map/ppermute | solution.py:21
  27.4 4.2 %copy.114 = f32[6,16,16,128]{2,1,3,0:T(8,128)} copy(f32[6,16,16,128]{3,2,1,0:T(8,128)S(1)} %copy-done.13) | data formatting | bytes 1572864 | tf_op args[5]
  32.4 10.4 %collective-permute-done.3 = f32[33,18,1]{2,1,0:T(8,128)} collective-permute-done((f32[33,18,1]{2,1,0:T(8,128)}, f32[33,18,1]{2,1,0:T(8,128)}, u32[]{:S(2)}, u32[]{:S(2)}) %collective-permute-start.3) | collective-permute-done | bytes 2408 | tf_op jit(solution)/shard_map/ppermute | solution.py:21
  44.9 2.0 %pad_maximum_fusion.14 = f32[16,17,130]{2,1,0:T(8,128)} fusion(f32[33,18,1]{2,1,0:T(8,128)} %collective-permute-done.3, f32[33,18,1]{2,1,0:T(8,128)S(1)} %collective-permute-done.2, f32[33,1,128]{2,1,0:T(1,128)} %copy-done.31, f32[33,1,128]{2,1,0:T(1,128)} %copy-done.33, f32[1,16,128]{2,1,0:T(8,128)} %copy-done.29, f32[16,16,128]{2,1,0:T(8,128)S(1)} %copy-done.15, ...), kind=kLoop, calls=%fused_computation.50 | loop fusion | flops 212160 | bytes 450320 | tf_op jit(solution)/shard_map/concatenate | solution.py:22
  46.9 5.1 %copy.115 = f32[6,16,1,128]{2,1,3,0:T(8,128)} copy(f32[6,16,1,128]{3,1,2,0:T(8,128)} %collective-permute-done.5) | data formatting | bytes 98304 | tf_op jit(solution)/shard_map/ppermute | solution.py:21
  52.0 4.9 %copy.113 = f32[6,16,1,128]{2,1,3,0:T(8,128)} copy(f32[6,16,1,128]{3,1,2,0:T(8,128)} %collective-permute-done.4) | data formatting | bytes 98304 | tf_op jit(solution)/shard_map/ppermute | solution.py:18
  56.8 8.2 %pad_maximum_fusion = f32[6,16,18,128]{2,1,3,0:T(8,128)S(1)} fusion(f32[6,16,1,128]{2,1,3,0:T(8,128)} %copy.115, f32[6,16,16,128]{2,1,3,0:T(8,128)} %copy.114, f32[6,16,1,128]{2,1,3,0:T(8,128)} %copy.113), kind=kLoop, calls=%fused_computation.1 | loop fusion | flops 442368 | bytes 1769472 | tf_op jit(solution)/shard_map/concatenate | solution.py:22
  65.1 2.6 %copy-done.1 = f32[6,16,18,128]{2,1,3,0:T(8,128)} copy-done((f32[6,16,18,128]{2,1,3,0:T(8,128)}, f32[6,16,18,128]{2,1,3,0:T(8,128)S(1)}, u32[]{:S(2)}) %copy-start.1) | copy-done | bytes 884760
  68.3 4.6 %collective-permute-start.7 = (f32[6,16,18,1]{2,1,3,0:T(8,128)}, f32[6,16,18,1]{2,1,3,0:T(8,128)}, u32[]{:S(2)}, u32[]{:S(2)}) collective-permute-start(f32[6,16,18,1]{2,1,3,0:T(8,128)} %get-tuple-element.6), channel_id=1, source_target_pairs={{1,0},{2,1},{3,2},{4,3},{5,4},{6,5},{7,6},{0,7},{9,8},{10,9},{11,1... | collective-permute-start | bytes 20744 | tf_op jit(solution)/shard_map/ppermute | solution.py:21
  73.4 4.8 %copy.117 = f32[6,16,18,128]{3,1,2,0:T(8,128)S(1)} copy(f32[6,16,18,128]{2,1,3,0:T(8,128)} %copy-done.1) | data formatting | bytes 1769472 | tf_op jit(solution)/shard_map/concatenate | solution.py:22
  78.2 2.5 %copy.119 = f32[6,16,18,1]{3,1,2,0:T(8,128)} copy(f32[6,16,18,1]{2,1,3,0:T(8,128)} %collective-permute-done.7) | data formatting | bytes 13824 | tf_op jit(solution)/shard_map/ppermute | solution.py:21
  80.7 2.4 %copy.116 = f32[6,16,18,1]{3,1,2,0:T(8,128)} copy(f32[6,16,18,1]{2,1,3,0:T(8,128)} %collective-permute-done.6) | data formatting | bytes 13824 | tf_op jit(solution)/shard_map/ppermute | solution.py:18
  83.1 2.3 %pad_maximum_fusion.3 = f32[6,16,18,130]{3,1,2,0:T(8,128)S(1)} fusion(f32[6,16,18,1]{3,1,2,0:T(8,128)} %copy.119, f32[6,16,18,128]{3,1,2,0:T(8,128)S(1)} %copy.117, f32[6,16,18,1]{3,1,2,0:T(8,128)} %copy.116), kind=kLoop, calls=%fused_computation.6 | loop fusion | flops 449280 | bytes 1797120 | tf_op jit(solution)/shard_map/concatenate | solution.py:22
  89.8 2.3 %collective-permute-done.8 = f32[6,16,1,128]{3,1,2,0:T(8,128)S(1)} collective-permute-done((f32[6,16,1,128]{3,1,2,0:T(8,128)S(1)}, f32[6,16,1,128]{3,1,2,0:T(8,128)S(1)}, u32[]{:S(2)}, u32[]{:S(2)}) %collective-permute-start.8) | collective-permute-done | bytes 49184 | tf_op jit(solution)/shard_map/ppermute | solution.py:18
  92.2 1.5 fusion.28
  93.8 1.8 copy.151
  95.6 4.9 %collective-permute-start.11 = (f32[6,16,18,1]{2,1,3,0:T(8,128)S(1)}, f32[6,16,18,1]{2,1,3,0:T(8,128)}, u32[]{:S(2)}, u32[]{:S(2)}) collective-permute-start(f32[6,16,18,1]{2,1,3,0:T(8,128)S(1)} %copy.151), channel_id=1, source_target_pairs={{1,0},{2,1},{3,2},{4,3},{5,4},{6,5},{7,6},{0,7},{9,8},{10,9},{11,1... | collective-permute-start | bytes 20744 | tf_op jit(solution)/shard_map/ppermute | solution.py:21
  100.5 2.4 %copy.150 = f32[6,16,18,1]{2,1,3,0:T(8,128)} copy(f32[6,16,18,1]{3,1,2,0:T(8,128)} %get-tuple-element.11) | data formatting | bytes 13824
  103.0 1.2 fusion.23
  104.1 2.5 %copy.128 = f32[6,16,18,1]{3,1,2,0:T(8,128)} copy(f32[6,16,18,1]{2,1,3,0:T(8,128)} %collective-permute-done.11) | data formatting | bytes 13824 | tf_op jit(solution)/shard_map/ppermute | solution.py:21
  106.6 3.5 %collective-permute-done.10 = f32[6,16,18,1]{2,1,3,0:T(8,128)} collective-permute-done((f32[6,16,18,1]{2,1,3,0:T(8,128)}, f32[6,16,18,1]{2,1,3,0:T(8,128)}, u32[]{:S(2)}, u32[]{:S(2)}) %collective-permute-start.10) | collective-permute-done | bytes 6944 | tf_op jit(solution)/shard_map/ppermute | solution.py:18
  110.0 2.4 %copy.126 = f32[6,16,18,1]{3,1,2,0:T(8,128)} copy(f32[6,16,18,1]{2,1,3,0:T(8,128)} %collective-permute-done.10) | data formatting | bytes 13824 | tf_op jit(solution)/shard_map/ppermute | solution.py:18
  112.5 2.2 %pad_maximum_fusion.5 = f32[6,16,18,130]{3,1,2,0:T(8,128)S(1)} fusion(f32[6,16,18,1]{3,1,2,0:T(8,128)} %copy.128, f32[6,16,1,128]{3,1,2,0:T(8,128)S(1)} %collective-permute-done.9, f32[6,16,16,128]{3,1,2,0:T(8,128)S(1)} %slice_subtract_fusion.6, f32[6,16,1,128]{3,1,2,0:T(8,128)} %copy-done.27, f32[6,16,18,1]{3,1,2,0:T(8,128)} %copy.126), kind=kLoop, calls=%fused_computation.9 | loop fusion | flops 898560 | bytes 1797120 | tf_op jit(solution)/shard_map/concatenate | solution.py:22
  116.8 1.9 slice_subtract_fusion.4
  120.4 1.5 gather_fusion
  121.9 1.3 collective-permute-done.12
  124.1 1.5 fusion.27
  125.6 1.8 copy.153
  127.4 1.5 collective-permute-start.15
  128.9 2.4 %copy.152 = f32[6,16,18,1]{2,1,3,0:T(8,128)} copy(f32[6,16,18,1]{3,1,2,0:T(8,128)} %get-tuple-element.9) | data formatting | bytes 13824
  131.9 2.6 %fusion.2 = f32[64,24,128]{2,1,0:T(8,128)} fusion(bf16[1,64,128,128]{3,2,1,0:T(8,128)(2,1)S(1)} %copy-done, bf16[64,24,128]{2,1,0:T(8,128)(2,1)} %gather_fusion, pred[64]{0:T(512)(128)(4,1)} %get-tuple-element.27, pred[64]{0:T(512)(128)(4,1)} %get-tuple-element.28), kind=kOutput, calls=%fused_computation.24 | convolution fusion | flops 50724864 | bytes 3276928 | tf_op jit(solution)/shard_map/fsb,sbc->sfc/dot_general | solution.py:78
  134.5 2.4 %reshape.178 = f32[32,2,3072]{2,1,0:T(2,128)} reshape(f32[64,24,128]{2,1,0:T(8,128)} %fusion.2) | data formatting | bytes 1572864 | tf_op jit(solution)/shard_map/reshape | solution.py:85
  137.0 1.7 copy.134
  138.6 2.4 %copy.132 = f32[6,16,18,1]{3,1,2,0:T(8,128)} copy(f32[6,16,18,1]{2,1,3,0:T(8,128)} %collective-permute-done.14) | data formatting | bytes 13824 | tf_op jit(solution)/shard_map/ppermute | solution.py:18
  141.0 2.2 %pad_maximum_fusion.7 = f32[6,16,18,130]{3,1,2,0:T(8,128)S(1)} fusion(f32[6,16,18,1]{3,1,2,0:T(8,128)} %copy.134, f32[6,16,1,128]{3,1,2,0:T(8,128)} %collective-permute-done.13, f32[6,16,16,128]{3,1,2,0:T(8,128)S(1)} %slice_subtract_fusion.4, f32[6,16,1,128]{3,1,2,0:T(8,128)} %collective-permute-done.12, f32[6,16,18,1]{3,1,2,0:T(8,128)} %copy.132), kind=kLoop, calls=%fused_computation.12 | loop fusion | flops 898560 | bytes 1797120 | tf_op jit(solution)/shard_map/concatenate | solution.py:22
  144.7 1.5 subtract_multiply_fusion.1
  146.2 1.6 slice_subtract_fusion.2
  147.8 5.0 %all-to-all-start.1 = ((f32[32,2,3072]{2,1,0:T(2,128)}), f32[32,2,3072]{2,1,0:T(2,128)}, u32[]{:S(2)}, u32[]{:S(2)}) async-start(f32[32,2,3072]{2,1,0:T(2,128)} %reshape.178), calls=%async_computation.1 | async-start | bytes 1572864 | tf_op jit(solution)/shard_map/all_to_all | solution.py:87
  153.6 1.5 collective-permute-start.17
  155.1 3.7 %collective-permute-done.17 = f32[6,16,1,128]{3,1,2,0:T(8,128)S(1)} collective-permute-done((f32[6,16,1,128]{3,1,2,0:T(8,128)S(1)}, f32[6,16,1,128]{3,1,2,0:T(8,128)S(1)}, u32[]{:S(2)}, u32[]{:S(2)}) %collective-permute-start.17) | collective-permute-done | bytes 49184 | tf_op jit(solution)/shard_map/ppermute | solution.py:21
  158.8 2.2 %collective-permute-done.16 = f32[6,16,1,128]{3,1,2,0:T(8,128)S(1)} collective-permute-done((f32[6,16,1,128]{3,1,2,0:T(8,128)S(1)}, f32[6,16,1,128]{3,1,2,0:T(8,128)S(1)}, u32[]{:S(2)}, u32[]{:S(2)}) %collective-permute-start.16) | collective-permute-done | bytes 49184 | tf_op jit(solution)/shard_map/ppermute | solution.py:18
  161.7 1.5 fusion.26
  163.2 2.4 %copy.155 = f32[6,16,18,1]{2,1,3,0:T(8,128)} copy(f32[6,16,18,1]{3,1,2,0:T(8,128)} %get-tuple-element.8) | data formatting | bytes 13824
  165.7 4.5 %collective-permute-start.19 = (f32[6,16,18,1]{2,1,3,0:T(8,128)}, f32[6,16,18,1]{2,1,3,0:T(8,128)}, u32[]{:S(2)}, u32[]{:S(2)}) collective-permute-start(f32[6,16,18,1]{2,1,3,0:T(8,128)} %copy.155), channel_id=1, source_target_pairs={{1,0},{2,1},{3,2},{4,3},{5,4},{6,5},{7,6},{0,7},{9,8},{10,9},{11,1... | collective-permute-start | bytes 20744 | tf_op jit(solution)/shard_map/ppermute | solution.py:21
  170.1 2.4 %copy.154 = f32[6,16,18,1]{2,1,3,0:T(8,128)} copy(f32[6,16,18,1]{3,1,2,0:T(8,128)} %get-tuple-element.7) | data formatting | bytes 13824
  173.1 1.9 reduce.7
  175.0 1.4 eq.25
  176.3 2.5 %copy.140 = f32[6,16,18,1]{3,1,2,0:T(8,128)} copy(f32[6,16,18,1]{2,1,3,0:T(8,128)} %collective-permute-done.19) | data formatting | bytes 13824 | tf_op jit(solution)/shard_map/ppermute | solution.py:21
  178.8 1.3 collective-permute-done.18
  180.1 2.4 %copy.138 = f32[6,16,18,1]{3,1,2,0:T(8,128)} copy(f32[6,16,18,1]{2,1,3,0:T(8,128)} %collective-permute-done.18) | data formatting | bytes 13824 | tf_op jit(solution)/shard_map/ppermute | solution.py:18
  182.5 2.2 %pad_maximum_fusion.9 = f32[6,16,18,130]{3,1,2,0:T(8,128)S(1)} fusion(f32[6,16,18,1]{3,1,2,0:T(8,128)} %copy.140, f32[6,16,1,128]{3,1,2,0:T(8,128)S(1)} %collective-permute-done.17, f32[6,16,16,128]{3,1,2,0:T(8,128)S(1)} %copy-done.3, f32[6,16,1,128]{3,1,2,0:T(8,128)} %copy-done.25, f32[6,16,18,1]{3,1,2,0:T(8,128)} %copy.138), kind=kLoop, calls=%fused_computation.15 | loop fusion | flops 898560 | bytes 1797120 | tf_op jit(solution)/shard_map/concatenate | solution.py:22
  184.7 1.6 subtract_multiply_fusion.4
  186.4 1.9 subtract_multiply_fusion
  188.3 2.6 %reshape.179 = f32[64,3072]{1,0:T(8,128)} reshape(f32[32,2,3072]{2,1,0:T(2,128)} %all-to-all-done.1) | data formatting | bytes 1572864 | tf_op jit(solution)/shard_map/reshape | solution.py:96
  190.9 1.6 fusion.5
  193.4 2.6 %fusion.8 = f32[6,16,16,128]{3,1,2,0:T(8,128)S(1)} fusion(f32[6,16,17,130]{3,1,2,0:T(8,128)} %subtract_multiply_fusion.4, f32[6,16,18,129]{3,1,2,0:T(8,128)S(1)} %copy-done.12, f32[6,16,16,128]{3,1,2,0:T(8,128)S(1)} %copy-done.3, f32[6,16,16,128]{3,1,0,2:T(8,128)S(1)} %bitcast.43, f32[16,128]{1,0:T(8,128)S(1)} %copy-done.35), kind=kLoop, calls=%fused_computation.32 | loop fusion | flops 1179648 | bytes 5513216 | tf_op jit(solution)/shard_map/add | solution.py:115
  196.0 1.1 copy.149
  (146 shorter events, 25.0 us)
Async XLA Ops:
  0.0 131.9 %copy-start = (bf16[1,64,128,128]{3,2,1,0:T(8,128)(2,1)S(1)}, bf16[1,64,128,128]{3,2,1,0:T(8,128)(2,1)}, u32[]{:S(2)}) copy-start(bf16[1,64,128,128]{3,2,1,0:T(8,128)(2,1)} %param.11) | copy-start | bytes 6291460
  0.0 27.4 %copy-start.13 = (f32[6,16,16,128]{3,2,1,0:T(8,128)S(1)}, f32[6,16,16,128]{3,2,1,0:T(8,128)}, u32[]{:S(2)}) copy-start(f32[6,16,16,128]{3,2,1,0:T(8,128)} %param.15) | copy-start | bytes 2359300
  2.0 44.9 %collective-permute-start.5 = (f32[6,16,1,128]{3,1,2,0:T(8,128)}, f32[6,16,1,128]{3,1,2,0:T(8,128)}, u32[]{:S(2)}, u32[]{:S(2)}) collective-permute-start(f32[6,16,1,128]{3,1,2,0:T(8,128)} %copy.169), channel_id=1, source_target_pairs={{8,0},{16,8},{24,16},{0,24},{9,1},{17,9},{25,17},{1,25},{10,2},{18... | collective-permute-start | bytes 147464 | tf_op jit(solution)/shard_map/ppermute | solution.py:21
  5.0 47.0 %collective-permute-start.4 = (f32[6,16,1,128]{3,1,2,0:T(8,128)}, f32[6,16,1,128]{3,1,2,0:T(8,128)}, u32[]{:S(2)}, u32[]{:S(2)}) collective-permute-start(f32[6,16,1,128]{3,1,2,0:T(8,128)} %copy.170), channel_id=1, source_target_pairs={{0,8},{8,16},{16,24},{24,0},{1,9},{9,17},{17,25},{25,1},{2,10},{10... | collective-permute-start | bytes 147464 | tf_op jit(solution)/shard_map/ppermute | solution.py:18
  6.3 20.5 %copy-start.29 = (f32[1,16,128]{2,1,0:T(8,128)}, f32[1,16,128]{2,1,0:T(8,128)S(1)}, u32[]{:S(2)}) copy-start(f32[1,16,128]{2,1,0:T(8,128)S(1)} %get-tuple-element.26) | copy-start | bytes 24580
  7.2 13.0 %collective-permute-start.1 = (f32[33,1,128]{2,1,0:T(1,128)S(1)}, f32[33,1,128]{2,1,0:T(1,128)S(1)}, u32[]{:S(2)}, u32[]{:S(2)}) collective-permute-start(f32[33,1,128]{2,1,0:T(1,128)S(1)} %get-tuple-element.24), channel_id=1, source_target_pairs={{8,0},{16,8},{24,16},{0,24},{9,1},{17,9},{25,17},{1,25},{10,2},{18... | collective-permute-start | bytes 50696 | tf_op jit(solution)/shard_map/ppermute | solution.py:21
  9.0 11.2 %collective-permute-start = (f32[33,1,128]{2,1,0:T(1,128)S(1)}, f32[33,1,128]{2,1,0:T(1,128)S(1)}, u32[]{:S(2)}, u32[]{:S(2)}) collective-permute-start(f32[33,1,128]{2,1,0:T(1,128)S(1)} %get-tuple-element.23), channel_id=1, source_target_pairs={{0,8},{8,16},{16,24},{24,0},{1,9},{9,17},{17,25},{25,1},{2,10},{10... | collective-permute-start | bytes 50696 | tf_op jit(solution)/shard_map/ppermute | solution.py:18
  12.4 135.4 %all-to-all-start = ((f32[32,1,2]{2,1,0:T(1,128)}), f32[32,1,2]{2,1,0:T(1,128)}, u32[]{:S(2)}, u32[]{:S(2)}) async-start(f32[32,1,2]{2,1,0:T(1,128)} %copy.144), calls=%async_computation | async-start | bytes 32768 | tf_op jit(solution)/shard_map/all_to_all | solution.py:88
  20.2 6.5 %copy-start.31 = (f32[33,1,128]{2,1,0:T(1,128)}, f32[33,1,128]{2,1,0:T(1,128)S(1)}, u32[]{:S(2)}) copy-start(f32[33,1,128]{2,1,0:T(1,128)S(1)} %collective-permute-done.1) | copy-start | bytes 50692
  20.2 6.5 %copy-start.33 = (f32[33,1,128]{2,1,0:T(1,128)}, f32[33,1,128]{2,1,0:T(1,128)S(1)}, u32[]{:S(2)}) copy-start(f32[33,1,128]{2,1,0:T(1,128)S(1)} %collective-permute-done) | copy-start | bytes 50692
  22.3 20.5 %collective-permute-start.3 = (f32[33,18,1]{2,1,0:T(8,128)}, f32[33,18,1]{2,1,0:T(8,128)}, u32[]{:S(2)}, u32[]{:S(2)}) collective-permute-start(f32[33,18,1]{2,1,0:T(8,128)} %get-tuple-element.22), channel_id=1, source_target_pairs={{1,0},{2,1},{3,2},{4,3},{5,4},{6,5},{7,6},{0,7},{9,8},{10,9},{11,1... | collective-permute-start | bytes 7136 | tf_op jit(solution)/shard_map/ppermute | solution.py:21
  26.8 16.1 %collective-permute-start.2 = (f32[33,18,1]{2,1,0:T(8,128)}, f32[33,18,1]{2,1,0:T(8,128)S(1)}, u32[]{:S(2)}, u32[]{:S(2)}) collective-permute-start(f32[33,18,1]{2,1,0:T(8,128)} %get-tuple-element.21), channel_id=1, source_target_pairs={{0,1},{1,2},{2,3},{3,4},{4,5},{5,6},{6,7},{7,0},{8,9},{9,10},{10,1... | collective-permute-start | bytes 7136 | tf_op jit(solution)/shard_map/ppermute | solution.py:18
  27.4 4.2 %copy-start.38 = (s32[1,32]{1,0:T(1,128)S(1)}, s32[1,32]{1,0:T(1,128)}, u32[]{:S(2)}) copy-start(s32[1,32]{1,0:T(1,128)} %param.14) | copy-start | bytes 388
  27.4 15.4 %copy-start.15 = (f32[16,16,128]{2,1,0:T(8,128)S(1)}, f32[16,16,128]{2,1,0:T(8,128)}, u32[]{:S(2)}) copy-start(f32[16,16,128]{2,1,0:T(8,128)} %param.17) | copy-start | bytes 393220
  27.4 15.4 %copy-start.16 = (f32[16,16,128]{2,1,0:T(8,128)S(1)}, f32[16,16,128]{2,1,0:T(8,128)}, u32[]{:S(2)}) copy-start(f32[16,16,128]{2,1,0:T(8,128)} %param.16) | copy-start | bytes 393220
  56.8 16.1 %copy-start.30 = (f32[1,16,128]{2,1,0:T(8,128)S(1)}, f32[1,16,128]{2,1,0:T(8,128)}, u32[]{:S(2)}) copy-start(f32[1,16,128]{2,1,0:T(8,128)} %copy-done.29) | copy-start | bytes 24580
  56.8 16.1 %copy-start.32 = (f32[33,1,128]{2,1,0:T(1,128)S(1)}, f32[33,1,128]{2,1,0:T(1,128)}, u32[]{:S(2)}) copy-start(f32[33,1,128]{2,1,0:T(1,128)} %copy-done.31) | copy-start | bytes 50692
  56.8 16.1 %copy-start.34 = (f32[33,1,128]{2,1,0:T(1,128)S(1)}, f32[33,1,128]{2,1,0:T(1,128)}, u32[]{:S(2)}) copy-start(f32[33,1,128]{2,1,0:T(1,128)} %copy-done.33) | copy-start | bytes 50692
  56.8 16.3 %copy-start.18 = (f32[16,17,130]{2,1,0:T(8,128)S(1)}, f32[16,17,130]{2,1,0:T(8,128)}, u32[]{:S(2)}) copy-start(f32[16,17,130]{2,1,0:T(8,128)} %pad_maximum_fusion.14) | copy-start | bytes 424324
  65.0 2.6 %copy-start.1 = (f32[6,16,18,128]{2,1,3,0:T(8,128)}, f32[6,16,18,128]{2,1,3,0:T(8,128)S(1)}, u32[]{:S(2)}) copy-start(f32[6,16,18,128]{2,1,3,0:T(8,128)S(1)} %pad_maximum_fusion) | copy-start | bytes 2654212
  68.3 9.9 %collective-permute-start.7 = (f32[6,16,18,1]{2,1,3,0:T(8,128)}, f32[6,16,18,1]{2,1,3,0:T(8,128)}, u32[]{:S(2)}, u32[]{:S(2)}) collective-permute-start(f32[6,16,18,1]{2,1,3,0:T(8,128)} %get-tuple-element.6), channel_id=1, source_target_pairs={{1,0},{2,1},{3,2},{4,3},{5,4},{6,5},{7,6},{0,7},{9,8},{10,9},{11,1... | collective-permute-start | bytes 20744 | tf_op jit(solution)/shard_map/ppermute | solution.py:21
  72.9 7.8 %collective-permute-start.6 = (f32[6,16,18,1]{2,1,3,0:T(8,128)}, f32[6,16,18,1]{2,1,3,0:T(8,128)}, u32[]{:S(2)}, u32[]{:S(2)}) collective-permute-start(f32[6,16,18,1]{2,1,3,0:T(8,128)} %get-tuple-element.5), channel_id=1, source_target_pairs={{0,1},{1,2},{2,3},{3,4},{4,5},{5,6},{6,7},{7,0},{8,9},{9,10},{10,1... | collective-permute-start | bytes 20744 | tf_op jit(solution)/shard_map/ppermute | solution.py:18
  83.1 2.3 %copy-start.8 = (f32[6,16,18,1]{3,1,2,0:T(8,128)S(1)}, f32[6,16,18,1]{3,1,2,0:T(8,128)}, u32[]{:S(2)}) copy-start(f32[6,16,18,1]{3,1,2,0:T(8,128)} %copy.119) | copy-start | bytes 20740
  83.1 2.3 %copy-start.11 = (f32[6,16,18,1]{3,1,2,0:T(8,128)S(1)}, f32[6,16,18,1]{3,1,2,0:T(8,128)}, u32[]{:S(2)}) copy-start(f32[6,16,18,1]{3,1,2,0:T(8,128)} %copy.116) | copy-start | bytes 20740
  83.1 2.3 %copy-start.19 = (f32[18,129]{1,0:T(8,128)S(1)}, f32[18,129]{1,0:T(8,128)}, u32[]{:S(2)}) copy-start(f32[18,129]{1,0:T(8,128)} %slice_multiply_fusion.1) | copy-start | bytes 27868
  85.4 0.7 copy-start.22
  86.2 1.1 copy-start.14
  87.3 1.3 copy-start.39
  87.3 1.3 copy-start.41
  88.0 27.1 %copy-start.2 = (f32[6,16,16,128]{3,1,2,0:T(8,128)}, f32[6,16,16,128]{3,1,2,0:T(8,128)S(1)}, u32[]{:S(2)}) copy-start(f32[6,16,16,128]{3,1,2,0:T(8,128)S(1)} %slice_subtract_fusion.6) | copy-start | bytes 2359300
  88.0 1.8 collective-permute-start.9
  88.1 4.1 %collective-permute-start.8 = (f32[6,16,1,128]{3,1,2,0:T(8,128)S(1)}, f32[6,16,1,128]{3,1,2,0:T(8,128)S(1)}, u32[]{:S(2)}, u32[]{:S(2)}) collective-permute-start(f32[6,16,1,128]{3,1,2,0:T(8,128)S(1)} %get-tuple-element.17), channel_id=1, source_target_pairs={{0,8},{8,16},{16,24},{24,0},{1,9},{9,17},{17,25},{25,1},{2,10},{10... | collective-permute-start | bytes 147464 | tf_op jit(solution)/shard_map/ppermute | solution.py:18
  92.1 1.6 copy-start.27
  95.6 8.6 %collective-permute-start.11 = (f32[6,16,18,1]{2,1,3,0:T(8,128)S(1)}, f32[6,16,18,1]{2,1,3,0:T(8,128)}, u32[]{:S(2)}, u32[]{:S(2)}) collective-permute-start(f32[6,16,18,1]{2,1,3,0:T(8,128)S(1)} %copy.151), channel_id=1, source_target_pairs={{1,0},{2,1},{3,2},{4,3},{5,4},{6,5},{7,6},{0,7},{9,8},{10,9},{11,1... | collective-permute-start | bytes 20744 | tf_op jit(solution)/shard_map/ppermute | solution.py:21
  102.9 7.1 %collective-permute-start.10 = (f32[6,16,18,1]{2,1,3,0:T(8,128)}, f32[6,16,18,1]{2,1,3,0:T(8,128)}, u32[]{:S(2)}, u32[]{:S(2)}) collective-permute-start(f32[6,16,18,1]{2,1,3,0:T(8,128)} %copy.150), channel_id=1, source_target_pairs={{0,1},{1,2},{2,3},{3,4},{4,5},{5,6},{6,7},{7,0},{8,9},{9,10},{10,1... | collective-permute-start | bytes 20744 | tf_op jit(solution)/shard_map/ppermute | solution.py:18
  112.5 2.2 %copy-start.23 = (f32[17,130]{1,0:T(8,128)S(1)}, f32[17,130]{1,0:T(8,128)}, u32[]{:S(2)}) copy-start(f32[17,130]{1,0:T(8,128)} %slice_multiply_fusion) | copy-start | bytes 26524
  114.7 1.2 copy-start.5
  114.7 1.4 copy-start.9
  114.7 1.4 copy-start.20
  114.7 1.4 copy-start.28
  116.8 3.0 %copy-start.40 = (s32[64]{0:T(128)S(1)}, s32[64]{0:T(128)}, u32[]{:S(2)}) copy-start(s32[64]{0:T(128)} %fusion.23) | copy-start | bytes 772
  116.8 3.6 %copy-start.17 = (bf16[24,16,128]{2,0,1:T(8,128)(2,1)S(1)}, bf16[24,16,128]{2,0,1:T(8,128)(2,1)}, u32[]{:S(2)}) copy-start(bf16[24,16,128]{2,0,1:T(8,128)(2,1)} %copy_bitcast_fusion) | copy-start | bytes 294916
  119.3 2.6 %collective-permute-start.13 = (f32[6,16,1,128]{3,1,2,0:T(8,128)}, f32[6,16,1,128]{3,1,2,0:T(8,128)}, u32[]{:S(2)}, u32[]{:S(2)}) collective-permute-start(f32[6,16,1,128]{3,1,2,0:T(8,128)} %get-tuple-element.16), channel_id=1, source_target_pairs={{8,0},{16,8},{24,16},{0,24},{9,1},{17,9},{25,17},{1,25},{10,2},{18... | collective-permute-start | bytes 147464 | tf_op jit(solution)/shard_map/ppermute | solution.py:21
  119.3 3.9 %collective-permute-start.12 = (f32[6,16,1,128]{3,1,2,0:T(8,128)}, f32[6,16,1,128]{3,1,2,0:T(8,128)}, u32[]{:S(2)}, u32[]{:S(2)}) collective-permute-start(f32[6,16,1,128]{3,1,2,0:T(8,128)} %get-tuple-element.15), channel_id=1, source_target_pairs={{0,8},{8,16},{16,24},{24,0},{1,9},{9,17},{17,25},{25,1},{2,10},{10... | collective-permute-start | bytes 147464 | tf_op jit(solution)/shard_map/ppermute | solution.py:18
  127.4 9.5 %collective-permute-start.15 = (f32[6,16,18,1]{2,1,3,0:T(8,128)S(1)}, f32[6,16,18,1]{2,1,3,0:T(8,128)S(1)}, u32[]{:S(2)}, u32[]{:S(2)}) collective-permute-start(f32[6,16,18,1]{2,1,3,0:T(8,128)S(1)} %copy.153), channel_id=1, source_target_pairs={{1,0},{2,1},{3,2},{4,3},{5,4},{6,5},{7,6},{0,7},{9,8},{10,9},{11,1... | collective-permute-start | bytes 20744 | tf_op jit(solution)/shard_map/ppermute | solution.py:21
  131.3 7.3 %collective-permute-start.14 = (f32[6,16,18,1]{2,1,3,0:T(8,128)}, f32[6,16,18,1]{2,1,3,0:T(8,128)}, u32[]{:S(2)}, u32[]{:S(2)}) collective-permute-start(f32[6,16,18,1]{2,1,3,0:T(8,128)} %copy.152), channel_id=1, source_target_pairs={{0,1},{1,2},{2,3},{3,4},{4,5},{5,6},{6,7},{7,0},{8,9},{9,10},{10,1... | collective-permute-start | bytes 20744 | tf_op jit(solution)/shard_map/ppermute | solution.py:18
  141.0 2.2 %copy-start.24 = (f32[17,130]{1,0:T(8,128)S(1)}, f32[17,130]{1,0:T(8,128)}, u32[]{:S(2)}) copy-start(f32[17,130]{1,0:T(8,128)} %slice_multiply_fusion) | copy-start | bytes 26524
  143.3 1.2 copy-start.6
  143.3 1.4 copy-start.10
  143.3 1.4 copy-start.21
  147.8 13.8 %copy-start.3 = (f32[6,16,16,128]{3,1,2,0:T(8,128)S(1)}, f32[6,16,16,128]{3,1,2,0:T(8,128)}, u32[]{:S(2)}) copy-start(f32[6,16,16,128]{3,1,2,0:T(8,128)} %slice_subtract_fusion.2) | copy-start | bytes 2359300
  147.8 40.5 %all-to-all-start.1 = ((f32[32,2,3072]{2,1,0:T(2,128)}), f32[32,2,3072]{2,1,0:T(2,128)}, u32[]{:S(2)}, u32[]{:S(2)}) async-start(f32[32,2,3072]{2,1,0:T(2,128)} %reshape.178), calls=%async_computation.1 | async-start | bytes 1572864 | tf_op jit(solution)/shard_map/all_to_all | solution.py:87
  153.6 5.2 %collective-permute-start.17 = (f32[6,16,1,128]{3,1,2,0:T(8,128)S(1)}, f32[6,16,1,128]{3,1,2,0:T(8,128)S(1)}, u32[]{:S(2)}, u32[]{:S(2)}) collective-permute-start(f32[6,16,1,128]{3,1,2,0:T(8,128)S(1)} %get-tuple-element.14), channel_id=1, source_target_pairs={{8,0},{16,8},{24,16},{0,24},{9,1},{17,9},{25,17},{1,25},{10,2},{18... | collective-permute-start | bytes 147464 | tf_op jit(solution)/shard_map/ppermute | solution.py:21
  155.1 5.9 %collective-permute-start.16 = (f32[6,16,1,128]{3,1,2,0:T(8,128)S(1)}, f32[6,16,1,128]{3,1,2,0:T(8,128)S(1)}, u32[]{:S(2)}, u32[]{:S(2)}) collective-permute-start(f32[6,16,1,128]{3,1,2,0:T(8,128)S(1)} %get-tuple-element.13), channel_id=1, source_target_pairs={{0,8},{8,16},{16,24},{24,0},{1,9},{9,17},{17,25},{25,1},{2,10},{10... | collective-permute-start | bytes 147464 | tf_op jit(solution)/shard_map/ppermute | solution.py:18
  161.0 0.6 copy-start.25
  165.7 10.7 %collective-permute-start.19 = (f32[6,16,18,1]{2,1,3,0:T(8,128)}, f32[6,16,18,1]{2,1,3,0:T(8,128)}, u32[]{:S(2)}, u32[]{:S(2)}) collective-permute-start(f32[6,16,18,1]{2,1,3,0:T(8,128)} %copy.155), channel_id=1, source_target_pairs={{1,0},{2,1},{3,2},{4,3},{5,4},{6,5},{7,6},{0,7},{9,8},{10,9},{11,1... | collective-permute-start | bytes 20744 | tf_op jit(solution)/shard_map/ppermute | solution.py:21
  172.6 7.5 %collective-permute-start.18 = (f32[6,16,18,1]{2,1,3,0:T(8,128)}, f32[6,16,18,1]{2,1,3,0:T(8,128)}, u32[]{:S(2)}, u32[]{:S(2)}) collective-permute-start(f32[6,16,18,1]{2,1,3,0:T(8,128)} %copy.154), channel_id=1, source_target_pairs={{0,1},{1,2},{2,3},{3,4},{4,5},{5,6},{6,7},{7,0},{8,9},{9,10},{10,1... | collective-permute-start | bytes 20744 | tf_op jit(solution)/shard_map/ppermute | solution.py:18
  184.7 1.6 copy-start.4
  184.7 1.7 copy-start.7
  184.7 1.7 copy-start.26
  186.4 4.5 %copy-start.37 = (f32[64]{0:T(128)S(1)}, f32[64]{0:T(128)}, u32[]{:S(2)}) copy-start(f32[64]{0:T(128)} %eq.25) | copy-start | bytes 772
  188.3 4.2 %copy-start.36 = (f32[96,24]{0,1:T(8,128)S(1)}, f32[96,24]{0,1:T(8,128)}, u32[]{:S(2)}) copy-start(f32[96,24]{0,1:T(8,128)} %param.19) | copy-start | bytes 27652
  188.3 5.1 %copy-start.35 = (f32[16,128]{1,0:T(8,128)S(1)}, f32[16,128]{1,0:T(8,128)}, u32[]{:S(2)}) copy-start(f32[16,128]{1,0:T(8,128)} %get-tuple-element.25) | copy-start | bytes 24580
  190.9 2.5 %copy-start.12 = (f32[6,16,18,129]{3,1,2,0:T(8,128)S(1)}, f32[6,16,18,129]{3,1,2,0:T(8,128)}, u32[]{:S(2)}) copy-start(f32[6,16,18,129]{3,1,2,0:T(8,128)} %subtract_multiply_fusion) | copy-start | bytes 2674948
where the time goes:
time: 199 us; the launch traced here: 197 us
  local copies, waits for them, and re-layouts  81.1 us (41%)
  other arithmetic  46.7 us (23%)
  starting transfers between devices  38.5 us (19%)
  waiting for transfers between devices  25.3 us (13%)
  matrix products  5.05 us (3%)
    unnamed x94, local copies, waits for them, and re-layouts  25.7 us
    ppermute x10, starting transfers between devices, extended_2(): lax.ppermute(lax.slice_in_dim(block, 0, width, axis=dim), axis, backward)  25.6 us
    concatenate x11, other arithmetic, extended_2(): block = jnp.concatenate([low, block, high], axis=dim)  21.4 us
    ppermute x10, waiting for transfers between devices, extended_2(): lax.ppermute(lax.slice_in_dim(block, 0, width, axis=dim), axis, backward)  14.7 us
    ppermute x5, local copies, waits for them, and re-layouts, extended_2(): lax.ppermute(lax.slice_in_dim(block, block.shape[dim] - width, None, axis...  14.5 us
    ppermute x5, local copies, waits for them, and re-layouts, extended_2(): lax.ppermute(lax.slice_in_dim(block, 0, width, axis=dim), axis, backward)  14.1 us
    ppermute x10, waiting for transfers between devices, extended_2(): lax.ppermute(lax.slice_in_dim(block, block.shape[dim] - width, None, axis...  10.6 us
    slice x9, local copies, waits for them, and re-layouts, extended_2(): lax.slice_in_dim(block, block.shape[dim] - width, None, axis=dim)  9.11 us
  transfers between devices with their start and end apart: 22, of which 9 were waited for; matrix products, arithmetic and copies ran while one was open for 59% of the time, Pallas kernels for 0%

commit v1 on v0

v1 whole, which is shorter than its diff:
```python
import functools

import jax
import jax.numpy as jnp
from jax import lax
from jax.experimental import pallas as pl
from jax.experimental.pallas import tpu as pltpu
from jax.sharding import PartitionSpec as P

NSUB = 4
DIFFUSION = 0.2
MESH = pl.DeviceIdType.MESH
F32 = jnp.float32


def offsets(step, n_lat, n_lon):
    ring = step // n_lat
    hop = (ring + 1) // 2
    d_lon = lax.rem(n_lon // 2 + jnp.where(ring % 2 == 1, -hop, hop) + n_lon, n_lon)
    d_lat = lax.rem(step + 1, n_lat)
    return d_lat, d_lon


def exchange_kernel(
    n_lat,
    n_lon,
    source_ref,
    target_ref,
    count_ref,
    atm_ref,
    weights_ref,
    tracers_ref,
    east_ref,
    north_ref,
    land_ref,
    flux_ref,
    rim_ref,
    rim_sea_ref,
    strip_ref,
    atm_blocks,
    weights,
    parts,
    arrived,
    marks,
    landed,
    sea,
    from_north,
    from_south,
    edge,
    from_east,
    from_west,
    weight_sem,
    part_send,
    part_recv,
    mark_send,
    mark_recv,
    lat_send,
    lat_recv,
    lon_send,
    lon_recv,
):
    lat, lon = lax.axis_index("lat"), lax.axis_index("lon")
    me = lat * n_lon + lon
    devices = n_lat * n_lon
    fields, block = atm_blocks.shape[1:]
    slots = marks.shape[1]
    levels, rows, cols = east_ref.shape
    tracer_count = tracers_ref.shape[0] // levels

    def partner(step):
        d_lat, d_lon = offsets(step, n_lat, n_lon)
        return lax.rem(lat + d_lat, n_lat), lax.rem(lon + d_lon, n_lon)

    def origin(step):
        d_lat, d_lon = offsets(step, n_lat, n_lon)
        return lax.rem(lat - d_lat + n_lat, n_lat) * n_lon + lax.rem(lon - d_lon + n_lon, n_lon)

    barrier = pltpu.get_barrier_semaphore()

    @pl.loop(0, devices - 1)
    def _(step):
        pl.semaphore_signal(barrier, inc=1, device_id=partner(step), device_id_type=MESH)

    def weight_copy(step):
        p_lat, p_lon = partner(step)
        tile = p_lat * n_lon + p_lon
        return pltpu.make_async_copy(
            weights_ref.at[pl.ds(tile * slots, slots)],
            weights.at[pl.ds(step * slots, slots)],
            weight_sem.at[step],
        )

    @pl.loop(0, devices)
    def _(step):
        weight_copy(step).start()

    for b in range(atm_blocks.shape[0]):
        atm_blocks[b] = atm_ref[:, b * block : (b + 1) * block].astype(F32)
    sea[...] = land_ref[...].astype(F32)

    @pl.loop(0, devices)
    def _(step):
        p_lat, p_lon = partner(step)
        tile = p_lat * n_lon + p_lon
        for k in range(slots):
            mark = jnp.where(k < count_ref[0, tile], target_ref[0, tile * slots + k], -1)
            marks[step, k] = jnp.full((1, block), mark, jnp.int32)

    pl.semaphore_wait(barrier, devices - 1)

    def lat_copies(north):
        first, to, into, way = (rows - 8, lat + 1, from_south, 0) if north else (0, lat - 1, from_north, 1)
        pieces = (
            (tracers_ref, into.at[pl.ds(0, tracer_count * levels)]),
            (east_ref, into.at[pl.ds(tracer_count * levels, levels)]),
            (north_ref, into.at[pl.ds((tracer_count + 1) * levels, levels)]),
        )
        copies = [
            pltpu.make_async_remote_copy(
                src_ref=ref.at[:, pl.ds(first, 8), :],
                dst_ref=dst,
                send_sem=lat_send.at[way, n],
                recv_sem=lat_recv.at[way, n],
                device_id=(to, lon),
                device_id_type=MESH,
            )
            for n, (ref, dst) in enumerate(pieces)
        ]
        copies.append(
            pltpu.make_async_remote_copy(
                src_ref=sea.at[pl.ds(first, 8), :],
                dst_ref=into.at[(tracer_count + 2) * levels],
                send_sem=lat_send.at[way, 3],
                recv_sem=lat_recv.at[way, 3],
                device_id=(to, lon),
                device_id_type=MESH,
            )
        )
        return copies

    @pl.when(lat < n_lat - 1)
    def _():
        for copy in lat_copies(True):
            copy.start()

    @pl.when(lat > 0)
    def _():
        for copy in lat_copies(False):
            copy.start()

    def mark_copy(step):
        return pltpu.make_async_remote_copy(
            src_ref=marks.at[step],
            dst_ref=landed.at[me],
            send_sem=mark_send.at[step],
            recv_sem=mark_recv.at[step],
            device_id=partner(step),
            device_id_type=MESH,
        )

    def part_copy(step):
        return pltpu.make_async_remote_copy(
            src_ref=parts.at[step],
            dst_ref=arrived.at[me],
            send_sem=part_send.at[step],
            recv_sem=part_recv.at[step],
            device_id=partner(step),
            device_id_type=MESH,
        )

    def remap(step, into, at):
        p_lat, p_lon = partner(step)
        tile = p_lat * n_lon + p_lon
        weight_copy(step).wait()
        for k in range(slots):
            chosen = atm_blocks[source_ref[0, tile * slots + k]].astype(jnp.bfloat16)
            into[at, k * fields : (k + 1) * fields, :] = jnp.dot(
                chosen, weights[step * slots + k], preferred_element_type=F32
            )

    @pl.loop(0, devices - 1)
    def _(step):
        mark_copy(step).start()

    def send(step):
        remap(step, parts, step)
        part_copy(step).start()

    half = devices // 2
    pl.loop(0, half)(send)

    planes = (tracer_count + 2) * levels + 1

    @pl.when(lat > 0)
    def _():
        for copy in lat_copies(True):
            copy.wait_recv()

    @pl.when(lat < n_lat - 1)
    def _():
        for copy in lat_copies(False):
            copy.wait_recv()

    @pl.when(lat == 0)
    def _():
        from_south[...] = jnp.zeros_like(from_south)

    @pl.when(lat == n_lat - 1)
    def _():
        from_north[...] = jnp.zeros_like(from_north)

    upper = lax.broadcasted_iota(jnp.int32, (8, cols), 0) < 4

    @pl.loop(0, planes - 1)
    def _(plane):
        rim_ref[plane] = jnp.where(upper, from_north[plane], from_south[plane])

    rim_sea_ref[...] = jnp.where(upper, from_north[planes - 1], from_south[planes - 1])

    width = cols // levels
    lane = lax.broadcasted_iota(jnp.int32, (rows + 8, cols), 1)
    groups = tracer_count + 3
    edge[...] = jnp.zeros_like(edge)

    @pl.loop(0, levels)
    def _(level):
        here = (lane >= level * width) & (lane < (level + 1) * width)
        shift = level * width + width // 2

        def put(group, inner, rim):
            moved = pltpu.roll(jnp.concatenate([inner, rim], axis=0), shift, 1)
            edge[group] = jnp.where(here, moved, edge[group])

        for t in range(tracer_count):
            put(t, tracers_ref[t * levels + level], rim_ref[t * levels + level])
        put(tracer_count, east_ref[level], rim_ref[tracer_count * levels + level])
        put(tracer_count + 1, north_ref[level], rim_ref[(tracer_count + 1) * levels + level])
        put(tracer_count + 2, sea[...], rim_sea_ref[...])

    def lon_copy(east):
        to, into, way = (lon + 1, from_west, 0) if east else (lon + n_lon - 1, from_east, 1)
        return pltpu.make_async_remote_copy(
            src_ref=edge,
            dst_ref=into,
            send_sem=lon_send.at[way],
            recv_sem=lon_recv.at[way],
            device_id=(lat, lax.rem(to, n_lon)),
            device_id_type=MESH,
        )

    lon_copy(True).start()
    lon_copy(False).start()

    pl.loop(half, devices - 1)(send)
    remap(devices - 1, arrived, me)
    landed[me] = marks[devices - 1]

    flux_ref[...] = jnp.zeros_like(flux_ref)

    def gather(source):
        for k in range(slots):
            mark = jnp.broadcast_to(landed[source, k], (8, block))
            for first in range(0, fields, 8):
                part = arrived[source, k * fields + first : k * fields + first + 8, :]
                for row in range(rows):
                    flux_ref[row, first : first + 8, :] += jnp.where(mark == row, part, 0.0)

    gather(me)

    lon_copy(True).wait_recv()
    lon_copy(False).wait_recv()
    west_side = lax.rem(lane, width) < width // 2

    @pl.loop(0, groups)
    def _(group):
        strip_ref[0, group] = jnp.where(west_side, edge[group], from_east[group])
        strip_ref[1, group] = jnp.where(west_side, from_west[group], edge[group])

    @pl.loop(0, devices - 1)
    def _(step):
        mark_copy(step).wait_recv()
        pltpu.make_async_remote_copy(
            src_ref=parts.at[step],
            dst_ref=arrived.at[origin(step)],
            send_sem=part_send.at[step],
            recv_sem=part_recv.at[step],
            device_id=partner(step),
            device_id_type=MESH,
        ).wait_recv()
        gather(origin(step))

    @pl.loop(0, devices - 1)
    def _(step):
        mark_copy(step).wait_send()
        part_copy(step).wait_send()

    @pl.when(lat < n_lat - 1)
    def _():
        for copy in lat_copies(True):
            copy.wait_send()

    @pl.when(lat > 0)
    def _():
        for copy in lat_copies(False):
            copy.wait_send()

    lon_copy(True).wait_send()
    lon_copy(False).wait_send()


def shifted(field):
    cols, rows = field.shape[1], field.shape[0]
    return (
        pltpu.roll(field, cols - 1, 1),
        pltpu.roll(field, 1, 1),
        pltpu.roll(field, rows - 1, 0),
        pltpu.roll(field, 1, 0),
    )


def faces(east, north, sea):
    sea_east = sea * pltpu.roll(sea, sea.shape[1] - 1, 1)
    sea_north = sea * pltpu.roll(sea, sea.shape[0] - 1, 0)
    return (
        sea_east * (0.5 * east + DIFFUSION),
        sea_east * (0.5 * east - DIFFUSION),
        sea_north * (0.5 * north + DIFFUSION),
        sea_north * (0.5 * north - DIFFUSION),
    )


def advect_kernel(
    tracers_ref,
    east_ref,
    north_ref,
    land_ref,
    rim_ref,
    rim_sea_ref,
    strip_ref,
    flux_ref,
    coupling_ref,
    out_ref,
    source,
    beyond,
    sides,
):
    levels, rows, cols = east_ref.shape
    tracer_count = tracers_ref.shape[0] // levels
    planes = tracer_count * levels
    width = cols // levels
    tall = (rows + 8, cols)
    lane = lax.broadcasted_iota(jnp.int32, tall, 1)
    place = lax.rem(lane, width)

    coupling = coupling_ref[...]
    lead = coupling.astype(jnp.bfloat16).astype(F32)
    factors = jnp.concatenate([lead, lead, coupling - lead], axis=1).astype(jnp.bfloat16)
    for row in range(rows):
        flux = flux_ref[row]
        head = flux.astype(jnp.bfloat16).astype(F32)
        stack = jnp.concatenate([head, flux - head, head], axis=0).astype(jnp.bfloat16)
        source[row * planes : (row + 1) * planes, :] = jnp.dot(
            factors, stack, preferred_element_type=F32
        )

    weights = []
    for side in range(2):
        sea = strip_ref[side, tracer_count + 2]
        a, b, c, d = faces(strip_ref[side, tracer_count], strip_ref[side, tracer_count + 1], sea)
        a_west, b_west = pltpu.roll(a, 1, 1), pltpu.roll(b, 1, 1)
        c_south, d_south = pltpu.roll(c, 1, 0), pltpu.roll(d, 1, 0)
        weights.append((1.0 - a + b_west - c + d_south, -b, a_west, -d, c_south))
        if side == 1:
            sides[0] = pltpu.roll(a, 1, 1)
            sides[1] = pltpu.roll(b, 1, 1)
        else:
            sides[2] = pltpu.roll(sea, cols - 1, 1)
    half = width // 2
    for t in range(tracer_count):
        now = [strip_ref[0, t], strip_ref[1, t]]
        for step in range(NSUB):
            east_of = pltpu.roll(now[0], cols - 1, 1)
            west_of = pltpu.roll(now[1], 1, 1)
            beyond[step, t] = jnp.where(place < half, east_of, west_of)
            if step < NSUB - 1:
                for side in range(2):
                    own, e, w, n, s = weights[side]
                    qe, qw, qn, qs = shifted(now[side])
                    now[side] = own * now[side] + e * qe + w * qw + n * qn + s * qs

    sea = jnp.concatenate([land_ref[...].astype(F32), rim_sea_ref[...]], axis=0)
    first, last = lane == 0, lane == cols - 1
    sea_here = sea[:rows]

    @pl.loop(0, levels)
    def _(level):
        shift = lax.rem(2 * cols - level * width - half, cols)
        east = jnp.concatenate([east_ref[level], rim_ref[planes + level]], axis=0)
        north = jnp.concatenate([north_ref[level], rim_ref[planes + levels + level]], axis=0)
        sea_beyond = pltpu.roll(sides[2], shift, 1)
        sea_east = sea * jnp.where(last, sea_beyond, pltpu.roll(sea, cols - 1, 1))
        _, _, c, d = faces(east, north, sea)
        a = sea_east * (0.5 * east + DIFFUSION)
        b = sea_east * (0.5 * east - DIFFUSION)
        a_west = jnp.where(first, pltpu.roll(sides[0], shift, 1), pltpu.roll(a, 1, 1))
        b_west = jnp.where(first, pltpu.roll(sides[1], shift, 1), pltpu.roll(b, 1, 1))
        c_south, d_south = pltpu.roll(c, 1, 0), pltpu.roll(d, 1, 0)
        own = 1.0 - a + b_west - c + d_south
        for t in range(tracer_count):
            plane = t * levels + level
            now = jnp.concatenate([tracers_ref[plane], rim_ref[plane]], axis=0)
            for step in range(NSUB):
                outer = pltpu.roll(beyond[step, t], shift, 1)
                qe, qw, qn, qs = shifted(now)
                qe, qw = jnp.where(last, outer, qe), jnp.where(first, outer, qw)
                now = own * now - b * qe + a_west * qw - d * qn + c_south * qs
            out_ref[plane] = now[:rows] + sea_here * source[pl.ds(plane, rows, planes), :]


def per_device(
    n_lat,
    n_lon,
    atm_fluxes,
    remap_weights,
    source_block,
    target_block,
    block_count,
    tracers,
    east_velocity,
    north_velocity,
    land_mask,
    coupling,
):
    fields, cells = atm_fluxes.shape
    block = remap_weights.shape[-1]
    devices = n_lat * n_lon
    slots = source_block.shape[1] // devices
    tracer_count, levels, rows, cols = tracers.shape
    planes = tracer_count * levels
    groups = tracer_count + 3
    tall = rows + 8
    flat = tracers.reshape(planes, rows, cols)
    vmem = pl.BlockSpec(memory_space=pltpu.VMEM)
    smem = pl.BlockSpec(memory_space=pltpu.SMEM)
    dma = pltpu.SemaphoreType.DMA
    shape = jax.ShapeDtypeStruct
    flux, rim, rim_sea, strip = pl.pallas_call(
        functools.partial(exchange_kernel, n_lat, n_lon),
        out_shape=(
            shape((rows, fields, block), F32),
            shape((planes + 2 * levels, 8, cols), F32),
            shape((8, cols), F32),
            shape((2, groups, tall, cols), F32),
        ),
        in_specs=[smem, smem, smem, vmem, pl.BlockSpec(memory_space=pl.ANY)] + [vmem] * 4,
        out_specs=(vmem,) * 4,
        scratch_shapes=[
            pltpu.VMEM((cells // block, fields, block), F32),
            pltpu.VMEM((devices * slots, block, block), jnp.bfloat16),
            pltpu.VMEM((devices, slots * fields, block), F32),
            pltpu.VMEM((devices, slots * fields, block), F32),
            pltpu.VMEM((devices, slots, 1, block), jnp.int32),
            pltpu.VMEM((devices, slots, 1, block), jnp.int32),
            pltpu.VMEM((rows, cols), F32),
            pltpu.VMEM((planes + 2 * levels + 1, 8, cols), F32),
            pltpu.VMEM((planes + 2 * levels + 1, 8, cols), F32),
            pltpu.VMEM((groups, tall, cols), F32),
            pltpu.VMEM((groups, tall, cols), F32),
            pltpu.VMEM((groups, tall, cols), F32),
            dma((devices,)),
            dma((devices,)),
            dma((devices,)),
            dma((devices,)),
            dma((devices,)),
            dma((2, 4)),
            dma((2, 4)),
            dma((2,)),
            dma((2,)),
        ],
        compiler_params=pltpu.CompilerParams(
            collective_id=0, has_side_effects=True, vmem_limit_bytes=40 * 1024 * 1024
        ),
    )(
        source_block,
        target_block,
        block_count,
        atm_fluxes,
        remap_weights.reshape(devices * slots, block, block),
        flat,
        east_velocity,
        north_velocity,
        land_mask,
    )
    out = pl.pallas_call(
        advect_kernel,
        out_shape=shape((planes, rows, cols), F32),
        in_specs=[vmem] * 9,
        out_specs=vmem,
        scratch_shapes=[
            pltpu.VMEM((rows * planes, cols), F32),
            pltpu.VMEM((NSUB, tracer_count, tall, cols), F32),
            pltpu.VMEM((3, tall, cols), F32),
        ],
        compiler_params=pltpu.CompilerParams(vmem_limit_bytes=40 * 1024 * 1024),
    )(flat, east_velocity, north_velocity, land_mask, rim, rim_sea, strip, flux, coupling)
    return out.reshape(tracers.shape)


def solution(mesh):
    placed = (
        P(None, ("lat", "lon")),
        P(("lat", "lon"), None, None, None),
        P(("lat", "lon"), None),
        P(("lat", "lon"), None),
        P(("lat", "lon"), None),
        P(None, None, "lat", "lon"),
        P(None, "lat", "lon"),
        P(None, "lat", "lon"),
        P("lat", "lon"),
        P(),
    )
    return jax.shard_map(
        functools.partial(per_device, mesh.shape["lat"], mesh.shape["lon"]),
        mesh=mesh,
        in_specs=placed,
        out_specs=P(None, None, "lat", "lon"),
        check_vma=False,
    )
```

time: 199 us -> 53.3 us (0.27)
  local copies, waits for them, and re-layouts: 81.1 us -> 8.87 us
  other arithmetic: 46.7 us -> 0 us
  Pallas kernels: 0 us -> 44 us
  starting transfers between devices: 38.5 us -> 0 us
  waiting for transfers between devices: 25.3 us -> 0 us
  matrix products: 5.05 us -> 0 us
    pallas_call x0 -> x2, Pallas kernels: none -> 44 us  [the longest x1 35.7 us: per_device(): pl.pallas_call(functools.partial(exchange_kernel, n_lat, n_lon), out_shap...]
    ppermute x10 -> x0, local copies, waits for them, and re-layouts: 28.6 us -> none  [the longest x5 14.5 us: extended_2(): lax.ppermute(lax.slice_in_dim(block, block.shape[dim] - width, None, axis...]
    ppermute x20 -> x0, starting transfers between devices: 27.3 us -> none  [the longest x10 25.6 us: extended_2(): lax.ppermute(lax.slice_in_dim(block, 0, width, axis=dim), axis, backward)]
    ppermute x20 -> x0, waiting for transfers between devices: 25.3 us -> none  [the longest x10 14.7 us: extended_2(): lax.ppermute(lax.slice_in_dim(block, 0, width, axis=dim), axis, backward)]
    concatenate x11 -> x0, other arithmetic: 21.4 us -> none  [extended_2(): block = jnp.concatenate([low, block, high], axis=dim)]
    unnamed x94 -> x19, local copies, waits for them, and re-layouts: 25.7 us -> 8.87 us
    all_to_all x2 -> x0, starting transfers between devices: 11.2 us -> none  [the longest x1 6.23 us: per_device(): lax.all_to_all(targets.reshape(tile_count, slot_count), ('lat', 'lon'), s...]
    slice x11 -> x0, local copies, waits for them, and re-layouts: 9.3 us -> none  [the longest x9 9.11 us: extended_2(): lax.slice_in_dim(block, block.shape[dim] - width, None, axis=dim)]
  transfers between devices with their start and end apart: 22 -> 0, of which waited for: 9 -> 0; matrix products, arithmetic and copies ran while one was open for 59% -> 0% of each run, Pallas kernels for 0% -> 0%
where the time goes in v1:
time: 53.3 us; the launch traced here: 52.9 us
  Pallas kernels  44 us (83%)
  local copies, waits for them, and re-layouts  8.87 us (17%)
    pallas_call x1, Pallas kernels, per_device(): pl.pallas_call(functools.partial(exchange_kernel, n_lat, n_lon), out_shap...  35.7 us
    unnamed x19, local copies, waits for them, and re-layouts  8.87 us
    pallas_call x1, Pallas kernels, per_device(): pl.pallas_call(advect_kernel, out_shape=shape((planes, rows, cols), F32),...  8.35 us

profile of v1, /device:TPU:0, one launch (start us, length us, event | category | flops | bytes accessed | tf_op | source)
XLA Modules:
  0.0 52.9 jit_solution(297893742382830796)
XLA Ops:
  0.0 0.8 %copy.11.coupling_ref = f32[96,24]{1,0:T(8,128)S(1)} copy(f32[96,24]{0,1:T(8,128)} %param.19) | data formatting | bytes 18432 | tf_op args[9]
  0.8 0.0 copy-start
  0.8 1.1 %copy-done = f32[6,16,16,128]{3,2,1,0:T(8,128)S(1)} copy-done((f32[6,16,16,128]{3,2,1,0:T(8,128)S(1)}, f32[6,16,16,128]{3,2,1,0:T(8,128)}, u32[]{:S(2)}) %copy-start) | copy-done | bytes 786456
  1.9 0.0 copy-start.1
  1.9 1.6 %copy-done.1 = bf16[1,64,128,128]{3,2,1,0:T(8,128)(2,1)S(1)} copy-done((bf16[1,64,128,128]{3,2,1,0:T(8,128)(2,1)S(1)}, bf16[1,64,128,128]{3,2,1,0:T(8,128)(2,1)}, u32[]{:S(2)}) %copy-start.1) | copy-done | bytes 2097176
  3.5 0.0 copy-start.2
  3.5 0.9 %copy-done.2 = f32[16,16,128]{2,1,0:T(8,128)S(1)} copy-done((f32[16,16,128]{2,1,0:T(8,128)S(1)}, f32[16,16,128]{2,1,0:T(8,128)}, u32[]{:S(2)}) %copy-start.2) | copy-done | bytes 131096
  4.4 0.0 copy-start.3
  4.4 0.9 %copy-done.3 = f32[16,16,128]{2,1,0:T(8,128)S(1)} copy-done((f32[16,16,128]{2,1,0:T(8,128)S(1)}, f32[16,16,128]{2,1,0:T(8,128)}, u32[]{:S(2)}) %copy-start.3) | copy-done | bytes 131096
  5.3 0.0 copy-start.4
  5.3 0.9 %copy-done.4 = bf16[24,2048]{1,0:T(8,128)(2,1)S(1)} copy-done((bf16[24,2048]{1,0:T(8,128)(2,1)S(1)}, bf16[24,2048]{1,0:T(8,128)(2,1)}, u32[]{:S(2)}) %copy-start.4) | copy-done | bytes 98328
  6.2 0.0 copy-start.5
  6.2 0.7 %copy-done.5 = s32[16,128]{1,0:T(8,128)S(1)} copy-done((s32[16,128]{1,0:T(8,128)S(1)}, s32[16,128]{1,0:T(8,128)}, u32[]{:S(2)}) %copy-start.5) | copy-done | bytes 8216
  6.9 0.0 copy-start.6
  6.9 0.7 %copy-done.6 = s32[1,64]{1,0:T(1,128)S(1)} copy-done((s32[1,64]{1,0:T(1,128)S(1)}, s32[1,64]{1,0:T(1,128)}, u32[]{:S(2)}) %copy-start.6) | copy-done | bytes 280
  7.6 0.0 copy-start.7
  7.6 0.7 %copy-done.7 = s32[1,64]{1,0:T(1,128)S(1)} copy-done((s32[1,64]{1,0:T(1,128)S(1)}, s32[1,64]{1,0:T(1,128)}, u32[]{:S(2)}) %copy-start.7) | copy-done | bytes 280
  8.2 0.0 copy-start.8
  8.2 0.7 %copy-done.8 = s32[1,32]{1,0:T(1,128)S(1)} copy-done((s32[1,32]{1,0:T(1,128)S(1)}, s32[1,32]{1,0:T(1,128)}, u32[]{:S(2)}) %copy-start.8) | copy-done | bytes 152
  8.9 35.7 %shard_map.100 = (f32[16,24,128]{2,1,0:T(8,128)S(1)}, f32[128,8,128]{2,1,0:T(8,128)S(1)}, f32[8,128]{1,0:T(8,128)S(1)}, f32[2,9,24,128]{3,2,1,0:T(8,128)S(1)}) custom-call(s32[1,64]{1,0:T(1,128)S(1)} %copy-done.6, s32[1,64]{1,0:T(1,128)S(1)} %copy-done.7, s32[1,32]{1,0:T(1,128)S(1)} %copy-done.8, bf16[24,2048]{1,0:T(8,128)(2,1)S(1)} %copy-done.4, ...), custom_call_target="tpu_custom_call" | custom-call | tf_op jit(solution)/shard_map/pallas_call | solution.py:447
  44.6 8.4 %shard_map.101 = f32[96,16,128]{2,1,0:T(8,128)} custom-call(f32[96,16,128]{2,1,0:T(8,128)S(1)} %bitcast.4, f32[16,16,128]{2,1,0:T(8,128)S(1)} %copy-done.2, f32[16,16,128]{2,1,0:T(8,128)S(1)} %copy-done.3, s32[16,128]{1,0:T(8,128)S(1)} %copy-done.5, f32[128,8,128]{2,1,0:T(8,128)S(1)} %get-tuple-element.9.rim_ref, ...), custom_call_target="tpu_custom_call" | custom-call | tf_op jit(solution)/shard_map/pallas_call | solution.py:494
Async XLA Ops:
  0.8 1.1 %copy-start = (f32[6,16,16,128]{3,2,1,0:T(8,128)S(1)}, f32[6,16,16,128]{3,2,1,0:T(8,128)}, u32[]{:S(2)}) copy-start(f32[6,16,16,128]{3,2,1,0:T(8,128)} %param.15) | copy-start | bytes 2359300
  1.9 1.6 %copy-start.1 = (bf16[1,64,128,128]{3,2,1,0:T(8,128)(2,1)S(1)}, bf16[1,64,128,128]{3,2,1,0:T(8,128)(2,1)}, u32[]{:S(2)}) copy-start(bf16[1,64,128,128]{3,2,1,0:T(8,128)(2,1)} %param.11) | copy-start | bytes 6291460
  3.5 0.9 %copy-start.2 = (f32[16,16,128]{2,1,0:T(8,128)S(1)}, f32[16,16,128]{2,1,0:T(8,128)}, u32[]{:S(2)}) copy-start(f32[16,16,128]{2,1,0:T(8,128)} %east_ref.3) | copy-start | bytes 393220
  4.4 0.9 %copy-start.3 = (f32[16,16,128]{2,1,0:T(8,128)S(1)}, f32[16,16,128]{2,1,0:T(8,128)}, u32[]{:S(2)}) copy-start(f32[16,16,128]{2,1,0:T(8,128)} %north_ref.3) | copy-start | bytes 393220
  5.3 0.9 %copy-start.4 = (bf16[24,2048]{1,0:T(8,128)(2,1)S(1)}, bf16[24,2048]{1,0:T(8,128)(2,1)}, u32[]{:S(2)}) copy-start(bf16[24,2048]{1,0:T(8,128)(2,1)} %atm_ref.1) | copy-start | bytes 294916
  6.2 0.7 %copy-start.5 = (s32[16,128]{1,0:T(8,128)S(1)}, s32[16,128]{1,0:T(8,128)}, u32[]{:S(2)}) copy-start(s32[16,128]{1,0:T(8,128)} %land_ref.3) | copy-start | bytes 24580
  6.9 0.7 %copy-start.6 = (s32[1,64]{1,0:T(1,128)S(1)}, s32[1,64]{1,0:T(1,128)}, u32[]{:S(2)}) copy-start(s32[1,64]{1,0:T(1,128)} %source_ref.1) | copy-start | bytes 772
  7.6 0.7 %copy-start.7 = (s32[1,64]{1,0:T(1,128)S(1)}, s32[1,64]{1,0:T(1,128)}, u32[]{:S(2)}) copy-start(s32[1,64]{1,0:T(1,128)} %target_ref.1) | copy-start | bytes 772
  8.2 0.7 %copy-start.8 = (s32[1,32]{1,0:T(1,128)S(1)}, s32[1,32]{1,0:T(1,128)}, u32[]{:S(2)}) copy-start(s32[1,32]{1,0:T(1,128)} %count_ref.1) | copy-start | bytes 388

commit v2 on v1

v2 whole, which is shorter than its diff:
```python
import functools

import jax
import jax.numpy as jnp
from jax import lax
from jax.experimental import pallas as pl
from jax.experimental.pallas import tpu as pltpu
from jax.sharding import PartitionSpec as P

NSUB = 4
DIFFUSION = 0.2
MESH = pl.DeviceIdType.MESH
F32 = jnp.float32


def offsets(step, n_lat, n_lon):
    ring = step // n_lat
    hop = (ring + 1) // 2
    d_lon = lax.rem(n_lon // 2 + jnp.where(ring % 2 == 1, -hop, hop) + n_lon, n_lon)
    d_lat = lax.rem(step + 1, n_lat)
    return d_lat, d_lon


def shifted(field):
    cols, rows = field.shape[1], field.shape[0]
    return (
        pltpu.roll(field, cols - 1, 1),
        pltpu.roll(field, 1, 1),
        pltpu.roll(field, rows - 1, 0),
        pltpu.roll(field, 1, 0),
    )


def faces(east, north, sea):
    sea_east = sea * pltpu.roll(sea, sea.shape[1] - 1, 1)
    sea_north = sea * pltpu.roll(sea, sea.shape[0] - 1, 0)
    return (
        sea_east * (0.5 * east + DIFFUSION),
        sea_east * (0.5 * east - DIFFUSION),
        sea_north * (0.5 * north + DIFFUSION),
        sea_north * (0.5 * north - DIFFUSION),
    )


def exchange_kernel(
    n_lat,
    n_lon,
    source_hbm,
    target_hbm,
    count_hbm,
    atm_hbm,
    weights_hbm,
    tracers_hbm,
    east_hbm,
    north_hbm,
    land_hbm,
    flux_ref,
    advected_hbm,
    source_ref,
    target_ref,
    count_ref,
    atm_ref,
    land_ref,
    advected_ref,
    atm_blocks,
    weights,
    parts,
    arrived,
    marks,
    landed,
    state,
    sea,
    to_north,
    to_south,
    from_north,
    from_south,
    edge,
    to_east,
    to_west,
    from_east,
    from_west,
    strip,
    beyond,
    sides,
    load_sem,
    weight_sem,
    part_send,
    part_recv,
    mark_send,
    mark_recv,
    lat_send,
    lat_recv,
    lon_send,
    lon_recv,
):
    lat, lon = lax.axis_index("lat"), lax.axis_index("lon")
    me = lat * n_lon + lon
    devices = n_lat * n_lon
    fields, block = atm_blocks.shape[1:]
    slots = marks.shape[1]
    planes, rows, cols = tracers_hbm.shape
    levels = east_hbm.shape[0]
    tracer_count = planes // levels
    total = planes + 2 * levels
    pairs = total // 2

    def partner(step):
        d_lat, d_lon = offsets(step, n_lat, n_lon)
        return lax.rem(lat + d_lat, n_lat), lax.rem(lon + d_lon, n_lon)

    def origin(step):
        d_lat, d_lon = offsets(step, n_lat, n_lon)
        return lax.rem(lat - d_lat + n_lat, n_lat) * n_lon + lax.rem(lon - d_lon + n_lon, n_lon)

    barrier = pltpu.get_barrier_semaphore()

    @pl.loop(0, devices - 1)
    def _(step):
        pl.semaphore_signal(barrier, inc=1, device_id=partner(step), device_id_type=MESH)

    inner = pl.ds(0, rows)
    loads = [
        pltpu.make_async_copy(a, b, load_sem.at[n])
        for n, (a, b) in enumerate(
            (
                (tracers_hbm, state.at[pl.ds(0, planes), inner, :]),
                (east_hbm, state.at[pl.ds(planes, levels), inner, :]),
                (north_hbm, state.at[pl.ds(planes + levels, levels), inner, :]),
                (land_hbm, land_ref),
                (source_hbm, source_ref),
                (target_hbm, target_ref),
                (count_hbm, count_ref),
                (atm_hbm, atm_ref),
            )
        )
    ]
    for load in loads:
        load.start()

    def weight_copy(step):
        p_lat, p_lon = partner(step)
        tile = p_lat * n_lon + p_lon
        return pltpu.make_async_copy(
            weights_hbm.at[pl.ds(tile * slots, slots)],
            weights.at[pl.ds(step * slots, slots)],
            weight_sem.at[step],
        )

    @pl.loop(0, devices)
    def _(step):
        weight_copy(step).start()

    for load in loads[:4]:
        load.wait()
    sea[0:rows, :] = land_ref[...].astype(F32)

    upper = lax.broadcasted_iota(jnp.int32, (8, cols), 0) < 4

    @pl.loop(0, pairs)
    def _(i):
        low, high = state[i, 0:8, :], state[i + pairs, 0:8, :]
        to_south[i] = jnp.where(upper, low, pltpu.roll(high, 4, 0))
        low, high = state[i, rows - 8 : rows, :], state[i + pairs, rows - 8 : rows, :]
        to_north[i] = jnp.where(upper, pltpu.roll(high, 4, 0), low)

    to_south[pairs] = sea[0:8, :]
    to_north[pairs] = sea[rows - 8 : rows, :]
    pl.semaphore_wait(barrier, devices - 1)

    def lat_copy(north):
        ref, into, to, way = (
            (to_north, from_south, lat + 1, 0) if north else (to_south, from_north, lat - 1, 1)
        )
        return pltpu.make_async_remote_copy(
            src_ref=ref,
            dst_ref=into,
            send_sem=lat_send.at[way],
            recv_sem=lat_recv.at[way],
            device_id=(to, lon),
            device_id_type=MESH,
        )

    @pl.when(lat < n_lat - 1)
    def _():
        lat_copy(True).start()

    @pl.when(lat > 0)
    def _():
        lat_copy(False).start()

    for load in loads[4:]:
        load.wait()
    for b in range(atm_blocks.shape[0]):
        atm_blocks[b] = atm_ref[:, b * block : (b + 1) * block].astype(F32)

    def mark_copy(step):
        return pltpu.make_async_remote_copy(
            src_ref=marks.at[step],
            dst_ref=landed.at[me],
            send_sem=mark_send.at[step],
            recv_sem=mark_recv.at[step],
            device_id=partner(step),
            device_id_type=MESH,
        )

    def part_copy(step):
        return pltpu.make_async_remote_copy(
            src_ref=parts.at[step],
            dst_ref=arrived.at[me],
            send_sem=part_send.at[step],
            recv_sem=part_recv.at[step],
            device_id=partner(step),
            device_id_type=MESH,
        )

    def remap(step, into, at):
        p_lat, p_lon = partner(step)
        tile = p_lat * n_lon + p_lon
        weight_copy(step).wait()
        for k in range(slots):
            mark = jnp.where(k < count_ref[0, tile], target_ref[0, tile * slots + k], -1)
            marks[step, k] = jnp.full((1, block), mark, jnp.int32)
            chosen = atm_blocks[source_ref[0, tile * slots + k]].astype(jnp.bfloat16)
            into[at, k * fields : (k + 1) * fields, :] = jnp.dot(
                chosen, weights[step * slots + k], preferred_element_type=F32
            )

    def send(step):
        remap(step, parts, step)
        mark_copy(step).start()
        part_copy(step).start()

    early = 3 * devices // 8
    pl.loop(0, early)(send)

    @pl.when(lat > 0)
    def _():
        lat_copy(True).wait_recv()

    @pl.when(lat < n_lat - 1)
    def _():
        lat_copy(False).wait_recv()

    @pl.when(lat == 0)
    def _():
        from_south[...] = jnp.zeros_like(from_south)

    @pl.when(lat == n_lat - 1)
    def _():
        from_north[...] = jnp.zeros_like(from_north)

    @pl.loop(0, pairs)
    def _(i):
        north, south = from_north[i], from_south[i]
        state[i, rows:, :] = jnp.where(upper, north, south)
        state[i + pairs, rows:, :] = pltpu.roll(jnp.where(upper, south, north), 4, 0)

    sea[rows:, :] = jnp.where(upper, from_north[pairs], from_south[pairs])

    width = cols // levels
    near = width // 2
    groups = tracer_count + 3
    joint = groups // 2
    lane = lax.broadcasted_iota(jnp.int32, (rows + 8, cols), 1)
    place = lax.rem(lane, width)
    west_side = place < near
    edge[...] = jnp.zeros_like(edge)

    @pl.loop(0, levels)
    def _(level):
        here = (lane >= level * width) & (lane < (level + 1) * width)
        shift = level * width + near
        for group in range(groups):
            field = state[group * levels + level] if group < groups - 1 else sea[...]
            edge[group] = jnp.where(here, pltpu.roll(field, shift, 1), edge[group])

    for group in range(joint):
        low, high = edge[group], edge[group + joint]
        to_east[group] = jnp.where(west_side, low, pltpu.roll(high, near, 1))
        to_west[group] = jnp.where(west_side, pltpu.roll(high, cols - near, 1), low)
    to_east[joint] = edge[groups - 1]
    to_west[joint] = edge[groups - 1]

    def lon_copy(east):
        ref, into, to, way = (
            (to_east, from_west, lon + 1, 0) if east else (to_west, from_east, lon + n_lon - 1, 1)
        )
        return pltpu.make_async_remote_copy(
            src_ref=ref,
            dst_ref=into,
            send_sem=lon_send.at[way],
            recv_sem=lon_recv.at[way],
            device_id=(lat, lax.rem(to, n_lon)),
            device_id_type=MESH,
        )

    lon_copy(True).start()
    lon_copy(False).start()

    pl.loop(early, devices - 1)(send)
    remap(devices - 1, arrived, me)
    landed[me] = marks[devices - 1]

    flux_ref[...] = jnp.zeros_like(flux_ref)

    def gather(source):
        seen = [jnp.broadcast_to(landed[source, k], (8, block)) for k in range(slots)]
        for first in range(0, fields, 8):
            part = [
                arrived[source, k * fields + first : k * fields + first + 8, :]
                for k in range(slots)
            ]
            for row in range(rows):
                added = flux_ref[row, first : first + 8, :]
                for k in range(slots):
                    added = added + jnp.where(seen[k] == row, part[k], 0.0)
                flux_ref[row, first : first + 8, :] = added

    gather(me)

    lon_copy(True).wait_recv()
    lon_copy(False).wait_recv()
    for group in range(joint):
        low, high = edge[group], edge[group + joint]
        east, west = from_east[group], from_west[group]
        strip[0, group] = jnp.where(west_side, low, east)
        strip[0, group + joint] = jnp.where(west_side, high, pltpu.roll(east, near, 1))
        strip[1, group] = jnp.where(west_side, west, low)
        strip[1, group + joint] = jnp.where(west_side, pltpu.roll(west, cols - near, 1), high)
    strip[0, groups - 1] = jnp.where(west_side, edge[groups - 1], from_east[joint])
    strip[1, groups - 1] = jnp.where(west_side, from_west[joint], edge[groups - 1])

    stencils = []
    for side in range(2):
        sea_strip = strip[side, groups - 1]
        a, b, c, d = faces(strip[side, tracer_count], strip[side, tracer_count + 1], sea_strip)
        a_west, b_west = pltpu.roll(a, 1, 1), pltpu.roll(b, 1, 1)
        c_south, d_south = pltpu.roll(c, 1, 0), pltpu.roll(d, 1, 0)
        stencils.append((1.0 - a + b_west - c + d_south, -b, a_west, -d, c_south))
        if side == 1:
            sides[0] = a_west
            sides[1] = b_west
        else:
            sides[2] = pltpu.roll(sea_strip, cols - 1, 1)

    @pl.loop(0, tracer_count)
    def _(t):
        now = [strip[0, t], strip[1, t]]
        for step in range(NSUB):
            east_of = pltpu.roll(now[0], cols - 1, 1)
            west_of = pltpu.roll(now[1], 1, 1)
            beyond[step, t] = jnp.where(west_side, east_of, west_of)
            if step < NSUB - 1:
                for side in range(2):
                    own, e, w, n, s = stencils[side]
                    qe, qw, qn, qs = shifted(now[side])
                    now[side] = own * now[side] + e * qe + w * qw + n * qn + s * qs

    first_lane, last_lane = lane == 0, lane == cols - 1
    sea_all = sea[...]

    @pl.loop(0, levels)
    def _(level):
        shift = lax.rem(2 * cols - level * width - near, cols)
        east, north = state[planes + level], state[planes + levels + level]
        sea_beyond = pltpu.roll(sides[2], shift, 1)
        sea_east = sea_all * jnp.where(last_lane, sea_beyond, pltpu.roll(sea_all, cols - 1, 1))
        _, _, c, d = faces(east, north, sea_all)
        a = sea_east * (0.5 * east + DIFFUSION)
        b = sea_east * (0.5 * east - DIFFUSION)
        a_west = jnp.where(first_lane, pltpu.roll(sides[0], shift, 1), pltpu.roll(a, 1, 1))
        b_west = jnp.where(first_lane, pltpu.roll(sides[1], shift, 1), pltpu.roll(b, 1, 1))
        c_south, d_south = pltpu.roll(c, 1, 0), pltpu.roll(d, 1, 0)
        own = 1.0 - a + b_west - c + d_south
        for t in range(tracer_count):
            now = state[t * levels + level]
            for step in range(NSUB):
                outer = pltpu.roll(beyond[step, t], shift, 1)
                qe, qw, qn, qs = shifted(now)
                qe, qw = jnp.where(last_lane, outer, qe), jnp.where(first_lane, outer, qw)
                now = own * now - b * qe + a_west * qw - d * qn + c_south * qs
            advected_ref[t * levels + level] = now[:rows]

    saved = pltpu.make_async_copy(advected_ref, advected_hbm, load_sem.at[0])
    saved.start()

    @pl.loop(0, devices - 1)
    def _(step):
        mark_copy(step).wait_recv()
        pltpu.make_async_remote_copy(
            src_ref=parts.at[step],
            dst_ref=arrived.at[origin(step)],
            send_sem=part_send.at[step],
            recv_sem=part_recv.at[step],
            device_id=partner(step),
            device_id_type=MESH,
        ).wait_recv()
        gather(origin(step))

    @pl.loop(0, devices - 1)
    def _(step):
        mark_copy(step).wait_send()
        part_copy(step).wait_send()

    @pl.when(lat < n_lat - 1)
    def _():
        lat_copy(True).wait_send()

    @pl.when(lat > 0)
    def _():
        lat_copy(False).wait_send()

    lon_copy(True).wait_send()
    lon_copy(False).wait_send()
    saved.wait()


def couple_kernel(
    flux_hbm,
    land_hbm,
    coupling_hbm,
    advected_hbm,
    out_ref,
    flux_ref,
    land_ref,
    coupling_ref,
    advected_ref,
    source,
    result,
    load_sem,
    sem,
):
    rows, cols = land_ref.shape
    planes = advected_ref.shape[0]
    pieces = sem.shape[0]
    share = planes // pieces
    loads = [
        pltpu.make_async_copy(a, b, load_sem.at[n])
        for n, (a, b) in enumerate(
            (
                (flux_hbm, flux_ref),
                (land_hbm, land_ref),
                (coupling_hbm, coupling_ref),
                (advected_hbm, advected_ref),
            )
        )
    ]
    for load in loads:
        load.start()
    for load in loads[:3]:
        load.wait()
    coupling = coupling_ref[...]
    lead = coupling.astype(jnp.bfloat16).astype(F32)
    factors = jnp.concatenate([lead, lead, coupling - lead], axis=0).astype(jnp.bfloat16)
    for row in range(rows):
        flux = flux_ref[row]
        head = flux.astype(jnp.bfloat16).astype(F32)
        stack = jnp.concatenate([head, flux - head, head], axis=0).astype(jnp.bfloat16)
        source[row * planes : (row + 1) * planes, :] = lax.dot_general(
            factors, stack, (((0,), (0,)), ((), ())), preferred_element_type=F32
        )
    sea = land_ref[...].astype(F32)
    loads[3].wait()
    copies = []
    for piece in range(pieces):
        for plane in range(piece * share, (piece + 1) * share):
            added = source[pl.ds(plane, rows, planes), :]
            result[plane] = advected_ref[plane] + sea * added
        here = pl.ds(piece * share, share)
        copies.append(pltpu.make_async_copy(result.at[here], out_ref.at[here], sem.at[piece]))
        copies[-1].start()
    for copy in copies:
        copy.wait()


def per_device(
    n_lat,
    n_lon,
    atm_fluxes,
    remap_weights,
    source_block,
    target_block,
    block_count,
    tracers,
    east_velocity,
    north_velocity,
    land_mask,
    coupling,
):
    fields, cells = atm_fluxes.shape
    block = remap_weights.shape[-1]
    devices = n_lat * n_lon
    slots = source_block.shape[1] // devices
    tracer_count, levels, rows, cols = tracers.shape
    planes = tracer_count * levels
    groups = tracer_count + 3
    tall = rows + 8
    pairs = planes // 2 + levels
    vmem = pl.BlockSpec(memory_space=pltpu.VMEM)
    anywhere = pl.BlockSpec(memory_space=pl.ANY)
    dma = pltpu.SemaphoreType.DMA
    shape = jax.ShapeDtypeStruct
    flux, advected = pl.pallas_call(
        functools.partial(exchange_kernel, n_lat, n_lon),
        out_shape=(
            shape((rows, fields, block), F32),
            shape((planes, rows, cols), F32),
        ),
        in_specs=[anywhere] * 9,
        out_specs=(vmem, anywhere),
        scratch_shapes=[
            pltpu.SMEM(source_block.shape, jnp.int32),
            pltpu.SMEM(target_block.shape, jnp.int32),
            pltpu.SMEM(block_count.shape, jnp.int32),
            pltpu.VMEM((fields, cells), jnp.bfloat16),
            pltpu.VMEM((rows, cols), jnp.int32),
            pltpu.VMEM((planes, rows, cols), F32),
            pltpu.VMEM((cells // block, fields, block), F32),
            pltpu.VMEM((devices * slots, block, block), jnp.bfloat16),
            pltpu.VMEM((devices, slots * fields, block), F32),
            pltpu.VMEM((devices, slots * fields, block), F32),
            pltpu.VMEM((devices, slots, 1, block), jnp.int32),
            pltpu.VMEM((devices, slots, 1, block), jnp.int32),
            pltpu.VMEM((planes + 2 * levels, tall, cols), F32),
            pltpu.VMEM((tall, cols), F32),
        ]
        + [pltpu.VMEM((pairs + 1, 8, cols), F32)] * 4
        + [pltpu.VMEM((groups, tall, cols), F32)]
        + [pltpu.VMEM((groups // 2 + 1, tall, cols), F32)] * 4
        + [
            pltpu.VMEM((2, groups, tall, cols), F32),
            pltpu.VMEM((NSUB, tracer_count, tall, cols), F32),
            pltpu.VMEM((3, tall, cols), F32),
            dma((8,)),
            dma((devices,)),
            dma((devices,)),
            dma((devices,)),
            dma((devices,)),
            dma((devices,)),
            dma((2,)),
            dma((2,)),
            dma((2,)),
            dma((2,)),
        ],
        compiler_params=pltpu.CompilerParams(
            collective_id=0, has_side_effects=True, vmem_limit_bytes=60 * 1024 * 1024
        ),
    )(
        source_block,
        target_block,
        block_count,
        atm_fluxes,
        remap_weights.reshape(devices * slots, block, block),
        tracers.reshape(planes, rows, cols),
        east_velocity,
        north_velocity,
        land_mask,
    )
    out = pl.pallas_call(
        couple_kernel,
        out_shape=shape((planes, rows, cols), F32),
        in_specs=[anywhere] * 4,
        out_specs=anywhere,
        scratch_shapes=[
            pltpu.VMEM((rows, fields, block), F32),
            pltpu.VMEM((rows, cols), jnp.int32),
            pltpu.VMEM((fields, planes), F32),
            pltpu.VMEM((planes, rows, cols), F32),
            pltpu.VMEM((rows * planes, cols), F32),
            pltpu.VMEM((planes, rows, cols), F32),
            dma((4,)),
            dma((tracer_count,)),
        ],
        compiler_params=pltpu.CompilerParams(vmem_limit_bytes=60 * 1024 * 1024),
    )(flux, land_mask, coupling.T, advected)
    return out.reshape(tracers.shape)


def solution(mesh):
    placed = (
        P(None, ("lat", "lon")),
        P(("lat", "lon"), None, None, None),
        P(("lat", "lon"), None),
        P(("lat", "lon"), None),
        P(("lat", "lon"), None),
        P(None, None, "lat", "lon"),
        P(None, "lat", "lon"),
        P(None, "lat", "lon"),
        P("lat", "lon"),
        P(),
    )
    return jax.shard_map(
        functools.partial(per_device, mesh.shape["lat"], mesh.shape["lon"]),
        mesh=mesh,
        in_specs=placed,
        out_specs=P(None, None, "lat", "lon"),
        check_vma=False,
    )
```

time: 53.3 us -> 37.9 us (0.71)
  the two profiles are of different devices: /device:TPU:0 before, /device:TPU:5 now
where the time goes in v2:
time: 37.9 us; the launch traced here: 37.7 us
  Pallas kernels  37.7 us (99%)
    pallas_call x1, Pallas kernels, per_device(): pl.pallas_call(functools.partial(exchange_kernel, n_lat, n_lon), out_shap...  35.2 us
    pallas_call x1, Pallas kernels, per_device(): pl.pallas_call(couple_kernel, out_shape=shape((planes, rows, cols), F32),...  2.5 us

profile of v2, /device:TPU:5, one launch (start us, length us, event | category | flops | bytes accessed | tf_op | source)
XLA Modules:
  0.0 37.7 jit_solution(17948186394405576981)
XLA Ops:
  0.0 35.2 %shard_map.100 = (f32[16,24,128]{2,1,0:T(8,128)}, f32[96,16,128]{2,1,0:T(8,128)}) custom-call(s32[1,64]{1,0:T(1,128)} %source_hbm.1, s32[1,64]{1,0:T(1,128)} %target_hbm.1, s32[1,32]{1,0:T(1,128)} %count_hbm.1, bf16[24,2048]{1,0:T(8,128)(2,1)} %atm_hbm.1, bf16[64,128,128]{2,1,0:T(8,128)(2,1)} %bitcast.4, f32[96,16,128]{2,1,0:T(8,128)} %bitcast.5, ...), custom_call_target="tpu_custom_call" | custom-call | tf_op jit(solution)/shard_map/pallas_call | solution.py:503
  35.2 2.5 %shard_map.101 = f32[96,16,128]{2,1,0:T(8,128)} custom-call(f32[16,24,128]{2,1,0:T(8,128)} %get-tuple-element.7.flux_hbm, s32[16,128]{1,0:T(8,128)} %land_hbm.3, f32[24,96]{1,0:T(8,128)} %bitcast.6, f32[96,16,128]{2,1,0:T(8,128)} %get-tuple-element.8.advected_hbm), custom_call_target="tpu_custom_call" | custom-call | tf_op jit(solution)/shard_map/pallas_call | solution.py:559

commit v3 on v2

--- a/solution.py
+++ b/solution.py
@@ -230,7 +230,7 @@
         mark_copy(step).start()
         part_copy(step).start()
 
-    early = 3 * devices // 8
+    early = devices // 8
     pl.loop(0, early)(send)
 
     @pl.when(lat > 0)

time: 37.9 us -> 37 us (0.976)
  Pallas kernels: 37.7 us -> 36.5 us
    pallas_call x1, Pallas kernels: 35.2 us -> 34 us  [per_device(): pl.pallas_call(functools.partial(exchange_kernel, n_lat, n_lon), out_shap...]
where the time goes in v3:
time: 37 us; the launch traced here: 36.5 us
  Pallas kernels  36.5 us (99%)
    pallas_call x1, Pallas kernels, per_device(): pl.pallas_call(functools.partial(exchange_kernel, n_lat, n_lon), out_shap...  34 us
    pallas_call x1, Pallas kernels, per_device(): pl.pallas_call(couple_kernel, out_shape=shape((planes, rows, cols), F32),...  2.5 us

profile of v3, /device:TPU:5, one launch (start us, length us, event | category | flops | bytes accessed | tf_op | source)
XLA Modules:
  0.0 36.5 jit_solution(9887956393317987002)
XLA Ops:
  0.0 34.0 %shard_map.100 = (f32[16,24,128]{2,1,0:T(8,128)}, f32[96,16,128]{2,1,0:T(8,128)}) custom-call(s32[1,64]{1,0:T(1,128)} %source_hbm.1, s32[1,64]{1,0:T(1,128)} %target_hbm.1, s32[1,32]{1,0:T(1,128)} %count_hbm.1, bf16[24,2048]{1,0:T(8,128)(2,1)} %atm_hbm.1, bf16[64,128,128]{2,1,0:T(8,128)(2,1)} %bitcast.4, f32[96,16,128]{2,1,0:T(8,128)} %bitcast.5, ...), custom_call_target="tpu_custom_call" | custom-call | tf_op jit(solution)/shard_map/pallas_call | solution.py:503
  34.0 2.5 %shard_map.101 = f32[96,16,128]{2,1,0:T(8,128)} custom-call(f32[16,24,128]{2,1,0:T(8,128)} %get-tuple-element.7.flux_hbm, s32[16,128]{1,0:T(8,128)} %land_hbm.3, f32[24,96]{1,0:T(8,128)} %bitcast.6, f32[96,16,128]{2,1,0:T(8,128)} %get-tuple-element.8.advected_hbm), custom_call_target="tpu_custom_call" | custom-call | tf_op jit(solution)/shard_map/pallas_call | solution.py:559

commit v4 on v3

--- a/solution.py
+++ b/solution.py
@@ -14,10 +14,10 @@
 
 
 def offsets(step, n_lat, n_lon):
-    ring = step // n_lat
+    ring = lax.rem(step, n_lon)
     hop = (ring + 1) // 2
     d_lon = lax.rem(n_lon // 2 + jnp.where(ring % 2 == 1, -hop, hop) + n_lon, n_lon)
-    d_lat = lax.rem(step + 1, n_lat)
+    d_lat = lax.rem(step // n_lon + 1, n_lat)
     return d_lat, d_lon
 
 

time: 37 us -> 36.3 us (0.981)
  the two profiles are of different devices: /device:TPU:5 before, /device:TPU:6 now
where the time goes in v4:
time: 36.3 us; the launch traced here: 36.1 us
  Pallas kernels  36.1 us (99%)
    pallas_call x1, Pallas kernels, per_device(): pl.pallas_call(functools.partial(exchange_kernel, n_lat, n_lon), out_shap...  33.6 us
    pallas_call x1, Pallas kernels, per_device(): pl.pallas_call(couple_kernel, out_shape=shape((planes, rows, cols), F32),...  2.5 us

profile of v4, /device:TPU:6, one launch (start us, length us, event | category | flops | bytes accessed | tf_op | source)
XLA Modules:
  0.0 36.1 jit_solution(8968865046355843234)
XLA Ops:
  0.0 33.6 %shard_map.100 = (f32[16,24,128]{2,1,0:T(8,128)}, f32[96,16,128]{2,1,0:T(8,128)}) custom-call(s32[1,64]{1,0:T(1,128)} %source_hbm.1, s32[1,64]{1,0:T(1,128)} %target_hbm.1, s32[1,32]{1,0:T(1,128)} %count_hbm.1, bf16[24,2048]{1,0:T(8,128)(2,1)} %atm_hbm.1, bf16[64,128,128]{2,1,0:T(8,128)(2,1)} %bitcast.4, f32[96,16,128]{2,1,0:T(8,128)} %bitcast.5, ...), custom_call_target="tpu_custom_call" | custom-call | tf_op jit(solution)/shard_map/pallas_call | solution.py:503
  33.6 2.5 %shard_map.101 = f32[96,16,128]{2,1,0:T(8,128)} custom-call(f32[16,24,128]{2,1,0:T(8,128)} %get-tuple-element.7.flux_hbm, s32[16,128]{1,0:T(8,128)} %land_hbm.3, f32[24,96]{1,0:T(8,128)} %bitcast.6, f32[96,16,128]{2,1,0:T(8,128)} %get-tuple-element.8.advected_hbm), custom_call_target="tpu_custom_call" | custom-call | tf_op jit(solution)/shard_map/pallas_call | solution.py:559

commit v5 on v4

--- a/solution.py
+++ b/solution.py
@@ -216,7 +216,6 @@
     def remap(step, into, at):
         p_lat, p_lon = partner(step)
         tile = p_lat * n_lon + p_lon
-        weight_copy(step).wait()
         for k in range(slots):
             mark = jnp.where(k < count_ref[0, tile], target_ref[0, tile * slots + k], -1)
             marks[step, k] = jnp.full((1, block), mark, jnp.int32)
@@ -225,13 +224,19 @@
                 chosen, weights[step * slots + k], preferred_element_type=F32
             )
 
-    def send(step):
-        remap(step, parts, step)
-        mark_copy(step).start()
-        part_copy(step).start()
-
-    early = devices // 8
-    pl.loop(0, early)(send)
+    def send(first, count):
+        steps = [first + n for n in range(count)]
+        for step in steps:
+            weight_copy(step).wait()
+        for step in steps:
+            remap(step, parts, step)
+        for step in steps:
+            mark_copy(step).start()
+            part_copy(step).start()
+
+    early = devices // 8 + 1
+    assert (devices - 1 - early) % 2 == 0
+    pl.loop(0, early)(lambda step: send(step, 1))
 
     @pl.when(lat > 0)
     def _():
@@ -297,7 +302,8 @@
     lon_copy(True).start()
     lon_copy(False).start()
 
-    pl.loop(early, devices - 1)(send)
+    pl.loop(0, (devices - 1 - early) // 2)(lambda pair: send(early + 2 * pair, 2))
+    weight_copy(devices - 1).wait()
     remap(devices - 1, arrived, me)
     landed[me] = marks[devices - 1]
 

time: 36.3 us -> 37.5 us (1.033)
  the two profiles are of different devices: /device:TPU:6 before, /device:TPU:5 now
where the time goes in v5:
time: 37.5 us; the launch traced here: 37.4 us
  Pallas kernels  37.4 us (100%)
    pallas_call x1, Pallas kernels, per_device(): pl.pallas_call(functools.partial(exchange_kernel, n_lat, n_lon), out_shap...  34.9 us
    pallas_call x1, Pallas kernels, per_device(): pl.pallas_call(couple_kernel, out_shape=shape((planes, rows, cols), F32),...  2.5 us

profile of v5, /device:TPU:5, one launch (start us, length us, event | category | flops | bytes accessed | tf_op | source)
XLA Modules:
  0.0 37.4 jit_solution(16689610094103613262)
XLA Ops:
  0.0 34.9 %shard_map.100 = (f32[16,24,128]{2,1,0:T(8,128)}, f32[96,16,128]{2,1,0:T(8,128)}) custom-call(s32[1,64]{1,0:T(1,128)} %source_hbm.1, s32[1,64]{1,0:T(1,128)} %target_hbm.1, s32[1,32]{1,0:T(1,128)} %count_hbm.1, bf16[24,2048]{1,0:T(8,128)(2,1)} %atm_hbm.1, bf16[64,128,128]{2,1,0:T(8,128)(2,1)} %bitcast.4, f32[96,16,128]{2,1,0:T(8,128)} %bitcast.5, ...), custom_call_target="tpu_custom_call" | custom-call | tf_op jit(solution)/shard_map/pallas_call | solution.py:509
  34.9 2.5 %shard_map.101 = f32[96,16,128]{2,1,0:T(8,128)} custom-call(f32[16,24,128]{2,1,0:T(8,128)} %get-tuple-element.7.flux_hbm, s32[16,128]{1,0:T(8,128)} %land_hbm.3, f32[24,96]{1,0:T(8,128)} %bitcast.6, f32[96,16,128]{2,1,0:T(8,128)} %get-tuple-element.8.advected_hbm), custom_call_target="tpu_custom_call" | custom-call | tf_op jit(solution)/shard_map/pallas_call | solution.py:565
